TPU v7x, 256 devices: a whole 4x4x8 slice. The times are simulated.
256 devices in a mesh: seq: 16 (over z, core), batch: 16 (over y, x).
Axes of the slice: x: 4, y: 4, z: 8, core: 2. Of those that a mesh axis runs over, the one named last changes fastest.
Arguments:
- features: bfloat16 [16, 2560, 1024], P('batch', 'seq'), may hold values from -6 to 6
- w_qk: bfloat16 [1024, 2048], replicated, may hold values from -0.1875 to 0.1875
- w_value: bfloat16 [1024, 1024], replicated, may hold values from -0.1875 to 0.1875
- w_gate: bfloat16 [1024, 1024], replicated, may hold values from -0.1875 to 0.1875
- cotangent: bfloat16 [16, 2560, 1024], P('batch', 'seq'), may hold values from -6 to 6
- lengths: int32 [16, 3], P('batch'), may hold values from 1 to 1280, 2560 in all within a row
Outputs:
- grad_qk_t: float32 [2048, 1024], P(('seq', 'batch'))
Inputs may be any that keep to these rules, and one draw needn't show every extreme that they name: The 3 lengths of a group sum to 2560, and the longest is exactly 1280.
All inputs are finite; a program needn't handle non-finite values.
Results may differ from a plain program's by a relative error of at most 0.0053.
Values may be sent and summed in bfloat16 or wider, within the bound.
No kernel may reach another device: no remote copies, remote signals or barrier semaphores. Data moves between devices by JAX's collectives and lax.ppermute only.
A program may use at most 128 MiB of HBM per device.

v0:
```python
import jax
import jax.numpy as jnp
from jax import lax
from jax.sharding import PartitionSpec as P

HEADS = 8


def silu_grad(z):
    s = jax.nn.sigmoid(z)
    return s * (1.0 + z * (1.0 - s))


def user_start(positions, begins, ends):
    inside = (positions[:, None] >= begins[None, :]) & (positions[:, None] < ends[None, :])
    return jnp.sum(jnp.where(inside, begins[None, :], 0), axis=1)


def pair_mask(query_pos, query_begin, key_pos):
    return (key_pos[None, :] <= query_pos[:, None]) & (key_pos[None, :] >= query_begin[:, None])


def body(features, w_qk, w_value, w_gate, cotangent, lengths):
    inputs = features[0]
    tok = inputs.shape[0]
    width = inputs.shape[1]
    head_dim = width // HEADS
    scale_factor = head_dim ** (-0.5)
    total = tok * lax.axis_size("seq")
    first = lax.axis_index("seq") * tok
    ends = jnp.cumsum(lengths[0])
    begins = ends - lengths[0]
    query_pos = first + jnp.arange(tok, dtype=jnp.int32)
    query_begin = user_start(query_pos, begins, ends)
    pre_qk = jnp.dot(inputs, w_qk, preferred_element_type=jnp.float32)
    pre_v = jnp.dot(inputs, w_value, preferred_element_type=jnp.float32)
    pre_u = jnp.dot(inputs, w_gate, preferred_element_type=jnp.float32)
    query = jax.nn.silu(pre_qk[:, :width]).astype(jnp.bfloat16)
    key = jax.nn.silu(pre_qk[:, width:]).astype(jnp.bfloat16)
    value = jax.nn.silu(pre_v).astype(jnp.bfloat16)
    gate = jax.nn.silu(pre_u)
    key_all, value_all = (
        lax.all_gather(key, "seq", axis=0, tiled=True),
        lax.all_gather(value, "seq", axis=0, tiled=True),
    )
    key_pos = jnp.arange(total, dtype=jnp.int32)
    mask = pair_mask(query_pos, query_begin, key_pos)
    q3 = query.reshape(tok, HEADS, head_dim)
    k3 = key_all.reshape(total, HEADS, head_dim)
    v3 = value_all.reshape(total, HEADS, head_dim)
    scores = jnp.einsum("qhd,khd->hqk", q3, k3, preferred_element_type=jnp.float32) * scale_factor
    weights = jnp.where(mask[None], jax.nn.silu(scores), 0.0).astype(jnp.bfloat16)
    attended = jnp.einsum("hqk,khd->qhd", weights, v3, preferred_element_type=jnp.float32).reshape(
        tok, width
    )
    mean = jnp.mean(attended, axis=-1, keepdims=True)
    centered = attended - mean
    rstd = lax.rsqrt(jnp.mean(centered * centered, axis=-1, keepdims=True) + 1e-05)
    normed = centered * rstd
    grad_normed = cotangent[0].astype(jnp.float32) * gate
    d_attended = rstd * (
        grad_normed
        - jnp.mean(grad_normed, axis=-1, keepdims=True)
        - normed * jnp.mean(grad_normed * normed, axis=-1, keepdims=True)
    )
    d_attended = d_attended.astype(jnp.bfloat16)
    d3 = d_attended.reshape(tok, HEADS, head_dim)
    d_weights = jnp.einsum("qhd,khd->hqk", d3, v3, preferred_element_type=jnp.float32)
    d_scores = (jnp.where(mask[None], d_weights * silu_grad(scores), 0.0) * scale_factor).astype(
        jnp.bfloat16
    )
    d_query = jnp.einsum("hqk,khd->qhd", d_scores, k3, preferred_element_type=jnp.float32).reshape(
        tok, width
    )
    key_terms = jnp.einsum(
        "hqk,qhd->khd", d_scores, q3, preferred_element_type=jnp.float32
    ).reshape(total, width)
    d_key = lax.psum_scatter(key_terms, "seq", scatter_dimension=0, tiled=True)
    d_pre = jnp.concatenate(
        [d_query * silu_grad(pre_qk[:, :width]), d_key * silu_grad(pre_qk[:, width:])], axis=1
    ).astype(jnp.bfloat16)
    return lax.psum_scatter(
        lax.dot_general(
            d_pre, inputs, (((0,), (0,)), ((), ())), preferred_element_type=jnp.float32
        ),
        ("seq", "batch"),
        scatter_dimension=0,
        tiled=True,
    )


def solution(mesh):
    return jax.shard_map(
        body,
        mesh=mesh,
        in_specs=(
            P("batch", "seq", None),
            P(),
            P(),
            P(),
            P("batch", "seq", None),
            P("batch", None),
        ),
        out_specs=P(("seq", "batch"), None),
        check_vma=False,
    )
```

profile of v0, /device:TPU:2, one launch (start us, length us, event | category | flops | bytes accessed | tf_op | source)
XLA Modules:
  0.0 1502.4 jit_solution(11743953525039291171)
XLA Ops:
  6.5 3.3 fusion.34
  9.8 1.2 fusion.40
  11.0 0.0 all-gather.5.cloned.1.call-start
  11.1 3.0 multiply_convert_fusion.4
  14.2 0.2 reduce-window.4
  14.4 0.1 select_reduce_fusion
  14.5 1.5 fusion.11
  16.0 41.4 %all-gather.3.cloned.1.call-done = bf16[2560,1024]{1,0:T(8,128)(2,1)} async-done(((bf16[160,1024]{1,0:T(8,128)(2,1)}), bf16[2560,1024]{1,0:T(8,128)(2,1)}) %all-gather.3.cloned.1.call-update) | async-done | bytes 5242896 | tf_op jit(solution)/shard_map/all_gather | solution.py:43
  57.5 9.2 fusion.3
  66.6 34.7 %all-gather.5.cloned.1.call-done = bf16[2560,1024]{1,0:T(8,128)(2,1)} async-done(((bf16[160,1024]{1,0:T(8,128)(2,1)}), bf16[2560,1024]{1,0:T(8,128)(2,1)}) %all-gather.5.cloned.1.call-update) | async-done | bytes 5242896 | tf_op jit(solution)/shard_map/all_gather | solution.py:44
  101.3 8.8 fusion.49
  110.1 0.2 fusion.22
  110.4 1.9 fusion.48
  112.3 0.3 fusion.23
  112.6 0.2 copy-done.6
  112.8 10.4 multiply_convert_fusion
  123.2 5.8 fusion.26
  129.0 11.4 copy.27
  140.4 0.2 reduce-scatter.5.cloned.1.call-start
  140.6 6.3 fusion.12
  146.9 66.8 %reduce-scatter.3.cloned.1.call-done = f32[160,1024]{1,0:T(8,128)} async-done(((f32[2560,1024]{1,0:T(8,128)}), f32[160,1024]{1,0:T(8,128)}) %reduce-scatter.3.cloned.1.call-update) | async-done | bytes 655376 | tf_op jit(solution)/shard_map/reduce_scatter | solution.py:78
  213.7 1.6 fusion.15
  215.2 5.6 fusion.17
  220.9 1274.9 %reduce-scatter.5.cloned.1.call-done = f32[8,1024]{1,0:T(8,128)} async-done(((f32[2048,1024]{1,0:T(8,128)}), f32[8,1024]{1,0:T(8,128)}) %reduce-scatter.5.cloned.1.call-update) | async-done | bytes 32784 | tf_op jit(solution)/shard_map/reduce_scatter | solution.py:82
  (26 shorter events, 0.2 us)
Async XLA Ops:
  6.5 103.8 %copy-start = (bf16[1024,1024]{1,0:T(8,128)(2,1)S(1)}, bf16[1024,1024]{1,0:T(8,128)(2,1)}, u32[]{:S(2)}) copy-start(bf16[1024,1024]{1,0:T(8,128)(2,1)} %param.9) | copy-start | bytes 6291460
  6.5 50.9 %all-gather.3.cloned.1.call-start = ((), (), s32[]{:S(2)}) async-start(), calls=%async_computation.2 | async-start | bytes 5570560 | tf_op jit(solution)/shard_map/all_gather | solution.py:43
  9.8 4.4 copy-start.7
  11.0 90.2 %all-gather.5.cloned.1.call-start = ((), (), s32[]{:S(2)}) async-start(), calls=%async_computation.3 | async-start | bytes 5570560 | tf_op jit(solution)/shard_map/all_gather | solution.py:44
  14.1 199.5 %reduce-scatter.3.cloned.1.call-start = ((), (), s32[]{:S(2)}) async-start(), calls=%async_computation.4 | async-start | bytes 11141120 | tf_op jit(solution)/shard_map/reduce_scatter | solution.py:78
  101.3 9.1 copy-start.4
  110.1 2.5 copy-start.5
  110.1 2.7 copy-start.6
  112.8 10.4 copy-start.3
  123.2 5.8 copy-start.2
  140.4 1355.4 %reduce-scatter.5.cloned.1.call-start = ((), (), s32[]{:S(2)}) async-start(), calls=%async_computation.5 | async-start | bytes 8421376 | tf_op jit(solution)/shard_map/reduce_scatter | solution.py:82
  215.2 1280.6 %copy-start.1 = (bf16[1024,1024]{1,0:T(8,128)(2,1)S(1)}, bf16[1024,1024]{1,0:T(8,128)(2,1)}, u32[]{:S(2)}) copy-start(bf16[1024,1024]{1,0:T(8,128)(2,1)} %param.9) | copy-start | bytes 6291460
Sparse Core Ops, SparseCore 0:
  11.2 46.2 all-gather.2
  59.3 41.9 all-gather.4
  140.5 73.1 reduce-scatter.2
  221.0 1274.7 reduce-scatter.4
where the time goes:
time: 1510 us; the launch traced here: 1500 us
  waiting for transfers between devices  1420 us (94%)
  matrix products  54.2 us (4%)
    reduce_scatter x1, waiting for transfers between devices, body(): lax.psum_scatter(lax.dot_general(d_pre, inputs, (((0,), (0,)), ((), ())),...  1270 us
    reduce_scatter x1, waiting for transfers between devices, body(): d_key = lax.psum_scatter(key_terms, 'seq', scatter_dimension=0, tiled=True)  66.8 us
    all_gather x1, waiting for transfers between devices, body(): lax.all_gather(key, 'seq', axis=0, tiled=True)  41.4 us
    all_gather x1, waiting for transfers between devices, body(): lax.all_gather(value, 'seq', axis=0, tiled=True)  34.7 us
  transfers between devices with their start and end apart: 4, of which 4 were waited for; matrix products, arithmetic and copies ran while one was open for 1% of the time, Pallas kernels for 0%

commit v1 on v0

v1 whole, which is shorter than its diff:
```python
import functools
import jax
import jax.numpy as jnp
from jax import lax
from jax.experimental import pallas as pl
from jax.experimental.pallas import tpu as pltpu
from jax.sharding import PartitionSpec as P

HEADS = 8
BLK = 256
F32 = jnp.float32
BF16 = jnp.bfloat16
VMEM_LIMIT = 56 * 1024 * 1024


def nn(a, b):
    return lax.dot_general(a, b, (((1,), (0,)), ((), ())), preferred_element_type=F32)


def nt(a, b):
    return lax.dot_general(a, b, (((1,), (1,)), ((), ())), preferred_element_type=F32)


def silu(z):
    half = 0.5 * z
    return half + half * jnp.tanh(half)


def silu_grad(z):
    half = 0.5 * z
    t = jnp.tanh(half)
    return 0.5 * (1.0 + t) * (1.0 + half * (1.0 - t))


def begin_of(pos, second, third):
    return jnp.where(pos >= third, third, jnp.where(pos >= second, second, 0))


def key_ranges(i, second, third):
    first = i * BLK
    low = begin_of(first, second, third) // BLK
    clear = (begin_of(first + BLK - 1, second, third) + BLK - 1) // BLK
    return low, jnp.minimum(jnp.maximum(clear, low), i)


def tile_mask(i, j, second, third):
    query = i * BLK + lax.broadcasted_iota(jnp.int32, (1, BLK), 1)
    begin = begin_of(query, second, third)
    key = j * BLK + lax.broadcasted_iota(jnp.int32, (BLK, BLK), 0)
    return (key <= query) & (key >= begin)


def forward_kernel(info, feats, wq, wk, wv, wu, cot, q_ref, k_ref, v_ref, qt_ref, kt_ref,
                   vt_ref, pre_ref, g_ref, att_ref, stat_ref, acc, *, scale):
    i = pl.program_id(0)
    role, second, third = info[1], info[2], info[3]
    rows = pl.ds(pl.multiple_of(i * BLK, BLK), BLK)
    x = feats[...]
    pre_q = nn(x, wq[...])
    pre_k = nn(x, wk[...])
    q = silu(pre_q).astype(BF16)
    k = silu(pre_k).astype(BF16)
    v = silu(nn(x, wv[...])).astype(BF16)
    gate = silu(nn(x, wu[...]))
    q_ref[rows, :] = q
    k_ref[rows, :] = k
    v_ref[rows, :] = v
    qt_ref[:, rows] = q.T
    kt_ref[:, rows] = k.T
    vt_ref[:, rows] = v.T
    pre_ref[:, rows] = jnp.where(role == 0, pre_q, pre_k).T
    g = (cot[...].astype(F32) * gate).T
    g_ref[:, rows] = g

    def tile(j, masked):
        keys = pl.ds(pl.multiple_of(j * BLK, BLK), BLK)
        half = nt(k_ref[keys, :], q) * (0.5 * scale)
        w = half + half * jnp.tanh(half)
        if masked:
            w = jnp.where(tile_mask(i, j, second, third), w, 0.0)
        acc[...] += nn(vt_ref[:, keys], w.astype(BF16))

    low, clear = key_ranges(i, second, third)
    acc[...] = jnp.zeros_like(acc)
    pl.loop(low, clear)(lambda j: tile(j, True))
    pl.loop(clear, i)(lambda j: tile(j, False))
    tile(i, True)
    att = acc[...]
    att_ref[:, rows] = att
    mean = jnp.mean(att, axis=0, keepdims=True)
    centered = att - mean
    stat_ref[0:1, rows] = mean
    stat_ref[1:2, rows] = jnp.sum(centered * centered, axis=0, keepdims=True)
    stat_ref[2:3, rows] = jnp.sum(g, axis=0, keepdims=True)
    stat_ref[3:4, rows] = jnp.sum(g * centered, axis=0, keepdims=True)


def backward_kernel(info, feats_hbm, q_ref, k_ref, v_ref, qt_ref, kt_ref, pre_ref, g_ref,
                    att_ref, stat_ref, out_ref, feats, datt, acc, sem, *, scale, width):
    role, second, third = info[1], info[2], info[3]
    total = q_ref.shape[0]
    blocks = total // BLK
    load = pltpu.make_async_copy(feats_hbm, feats, sem)
    load.start()
    mean = stat_ref[0:1, :]
    rstd = lax.rsqrt(stat_ref[1:2, :] / width + 1e-5)
    g_mean = stat_ref[2:3, :] / width
    gn_mean = stat_ref[3:4, :] * rstd / width
    normed = (att_ref[...] - mean) * rstd
    datt[...] = (rstd * (g_ref[...] - g_mean - normed * gn_mean)).astype(BF16)

    def d_scores(i, j, masked):
        queries = pl.ds(pl.multiple_of(i * BLK, BLK), BLK)
        keys = pl.ds(pl.multiple_of(j * BLK, BLK), BLK)
        half = nt(k_ref[keys, :], q_ref[queries, :]) * (0.5 * scale)
        dw = nn(v_ref[keys, :], datt[:, queries])
        t = jnp.tanh(half)
        ds = (1.0 + t) * (1.0 + half * (1.0 - t)) * dw
        if masked:
            ds = jnp.where(tile_mask(i, j, second, third), ds, 0.0)
        return ds.astype(BF16)

    acc[...] = jnp.zeros_like(acc)

    def query_tile(i, j, masked):
        queries = pl.ds(pl.multiple_of(i * BLK, BLK), BLK)
        keys = pl.ds(pl.multiple_of(j * BLK, BLK), BLK)
        acc[:, queries] += nn(kt_ref[:, keys], d_scores(i, j, masked))

    def key_tile(i, j, masked):
        queries = pl.ds(pl.multiple_of(i * BLK, BLK), BLK)
        keys = pl.ds(pl.multiple_of(j * BLK, BLK), BLK)
        acc[:, keys] += nt(qt_ref[:, queries], d_scores(i, j, masked))

    def sweep(tile):
        @pl.loop(0, blocks)
        def _(i):
            low, clear = key_ranges(i, second, third)
            pl.loop(low, clear)(lambda j: tile(i, j, True))
            pl.loop(clear, i)(lambda j: tile(i, j, False))
            tile(i, i, True)

    pl.when(role == 0)(lambda: sweep(query_tile))
    pl.when(role == 1)(lambda: sweep(key_tile))
    dpre = (acc[...] * (0.5 * scale) * silu_grad(pre_ref[...])).astype(BF16)
    load.wait()
    out_ref[...] = nn(dpre, feats[...]).astype(out_ref.dtype)


def body(features, w_qk, w_value, w_gate, cotangent, lengths):
    inputs = features[0]
    tok, width = inputs.shape
    n_seq = lax.axis_size("seq")
    n_batch = lax.axis_size("batch")
    total = tok * n_seq
    dim = width // HEADS
    scale = dim ** (-0.5)
    s = lax.axis_index("seq")
    head, role = s % HEADS, s // HEADS
    info = jnp.stack([head, role, lengths[0, 0], lengths[0, 0] + lengths[0, 1]]).astype(jnp.int32)
    feats = lax.all_gather(inputs, "seq", axis=0, tiled=True)
    pieces = jnp.moveaxis(cotangent[0].reshape(tok, HEADS, dim), 1, 0)
    pieces = jnp.concatenate([pieces, pieces], axis=0)
    cot = lax.all_to_all(pieces, "seq", 0, 0).reshape(total, dim)

    blocks = total // BLK
    whole = lambda shape: pl.BlockSpec(shape, lambda i, info: (0, 0))
    row = jax.ShapeDtypeStruct((total, dim), BF16)
    col = jax.ShapeDtypeStruct((dim, total), BF16)
    colf = jax.ShapeDtypeStruct((dim, total), F32)
    stat = jax.ShapeDtypeStruct((4, total), F32)
    q, k, v, qt, kt, vt, pre, g, att, stats = pl.pallas_call(
        functools.partial(forward_kernel, scale=scale),
        grid_spec=pltpu.PrefetchScalarGridSpec(
            num_scalar_prefetch=1,
            grid=(blocks,),
            in_specs=[
                pl.BlockSpec((BLK, width), lambda i, info: (i, 0)),
                pl.BlockSpec((width, dim), lambda i, info: (0, info[0])),
                pl.BlockSpec((width, dim), lambda i, info: (0, HEADS + info[0])),
                pl.BlockSpec((width, dim), lambda i, info: (0, info[0])),
                pl.BlockSpec((width, dim), lambda i, info: (0, info[0])),
                pl.BlockSpec((BLK, dim), lambda i, info: (i, 0)),
            ],
            out_specs=[whole(a.shape) for a in (row, row, row, col, col, col, colf, colf, colf, stat)],
            scratch_shapes=[pltpu.VMEM((dim, BLK), F32)],
        ),
        out_shape=[row, row, row, col, col, col, colf, colf, colf, stat],
        compiler_params=pltpu.CompilerParams(vmem_limit_bytes=VMEM_LIMIT),
        name="forward",
    )(info, feats, w_qk, w_qk, w_value, w_gate, cot)

    count = dim
    for step in (1, 2, 4):
        other = lax.ppermute(stats, "seq", [(a, a ^ step) for a in range(n_seq)])
        delta = stats[0] - other[0]
        stats = jnp.stack([
            0.5 * (stats[0] + other[0]),
            stats[1] + other[1] + delta * delta * (0.5 * count),
            stats[2] + other[2],
            stats[3] + other[3] + 0.5 * delta * (stats[2] - other[2]),
        ])
        count = 2 * count

    vmem = pl.BlockSpec(memory_space=pltpu.VMEM)
    part = pl.pallas_call(
        functools.partial(backward_kernel, scale=scale, width=width),
        in_specs=[pl.BlockSpec(memory_space=pltpu.SMEM), pl.BlockSpec(memory_space=pl.ANY)] + [vmem] * 9,
        out_specs=vmem,
        out_shape=jax.ShapeDtypeStruct((dim, width), BF16),
        scratch_shapes=[
            pltpu.VMEM((total, width), BF16),
            pltpu.VMEM((dim, total), BF16),
            pltpu.VMEM((dim, total), F32),
            pltpu.SemaphoreType.DMA,
        ],
        compiler_params=pltpu.CompilerParams(vmem_limit_bytes=VMEM_LIMIT),
        name="backward",
    )(info, feats, q, k, v, qt, kt, pre, g, att, stats)
    parts = lax.all_to_all(part.reshape(n_batch, dim // n_batch, width), "batch", 0, 0)
    return jnp.sum(parts.astype(F32), axis=0)


def solution(mesh):
    return jax.shard_map(
        body,
        mesh=mesh,
        in_specs=(
            P("batch", "seq", None),
            P(),
            P(),
            P(),
            P("batch", "seq", None),
            P("batch", None),
        ),
        out_specs=P(("seq", "batch"), None),
        check_vma=False,
    )
```

time: 1510 us -> 147 us (0.10)
  waiting for transfers between devices: 1420 us -> 52.7 us
  matrix products: 54.2 us -> 0 us
  Pallas kernels: 0 us -> 44 us
  blocking collectives: 0 us -> 19 us
    reduce_scatter x2 -> x0, waiting for transfers between devices: 1340 us -> none  [the longest x1 1270 us: body(): lax.psum_scatter(lax.dot_general(d_pre, inputs, (((0,), (0,)), ((), ())),...]
    dot_general x9 -> x0, matrix products: 54.2 us -> none  [the longest x1 10.4 us: body(): jnp.einsum('qhd,khd->hqk', d3, v3, preferred_element_type=jnp.float32)]
    all_gather x2 -> x1, waiting for transfers between devices: 76.1 us -> 25.4 us  [body(): feats = lax.all_gather(inputs, 'seq', axis=0, tiled=True)]
    pallas_call x0 -> x2, Pallas kernels: none -> 44 us  [the longest x1 24.8 us: body(): pl.pallas_call(functools.partial(forward_kernel, scale=scale), grid_spec=...]
    all_to_all x0 -> x1, blocking collectives: none -> 19 us  [body(): lax.all_to_all(part.reshape(n_batch, dim // n_batch, width), 'batch', 0, 0)]
    all_to_all x0 -> x1, waiting for transfers between devices: none -> 18.4 us  [body(): cot = lax.all_to_all(pieces, 'seq', 0, 0).reshape(total, dim)]
  transfers between devices with their start and end apart: 4 -> 5, of which waited for: 4 -> 5; matrix products, arithmetic and copies ran while one was open for 1% -> 3% of each run, Pallas kernels for 0% -> 0%
where the time goes in v1:
time: 147 us; the launch traced here: 148 us
  waiting for transfers between devices  52.7 us (36%)
  Pallas kernels  44 us (30%)
  blocking collectives  19 us (13%)
  between operations  14.8 us (10%)
  starting transfers between devices  11.3 us (8%)
  other arithmetic  4.71 us (3%)
  local copies, waits for them, and re-layouts  1.67 us (1%)
    all_gather x1, waiting for transfers between devices, body(): feats = lax.all_gather(inputs, 'seq', axis=0, tiled=True)  25.4 us
    pallas_call x1, Pallas kernels, body(): pl.pallas_call(functools.partial(forward_kernel, scale=scale), grid_spec=...  24.8 us
    pallas_call x1, Pallas kernels, body(): pl.pallas_call(functools.partial(backward_kernel, scale=scale, width=widt...  19.2 us
    all_to_all x1, blocking collectives, body(): lax.all_to_all(part.reshape(n_batch, dim // n_batch, width), 'batch', 0, 0)  19 us
    all_to_all x1, waiting for transfers between devices, body(): cot = lax.all_to_all(pieces, 'seq', 0, 0).reshape(total, dim)  18.4 us
    all_to_all x1, starting transfers between devices, body(): cot = lax.all_to_all(pieces, 'seq', 0, 0).reshape(total, dim)  8.57 us
    ppermute x3, waiting for transfers between devices, body(): other = lax.ppermute(stats, 'seq', [(a, a ^ step) for a in range(n_seq)])  8.21 us
  transfers between devices with their start and end apart: 5, of which 5 were waited for; matrix products, arithmetic and copies ran while one was open for 3% of the time, Pallas kernels for 0%

profile of v1, /device:TPU:2, one launch (start us, length us, event | category | flops | bytes accessed | tf_op | source)
XLA Modules:
  0.0 148.1 jit_solution(11472478961625968457)
XLA Ops:
  6.5 0.0 all-gather.3.cloned.1.call-start
  6.5 0.7 all-gather.3.cloned.1.call-update
  7.3 1.0 copy.8
  8.3 0.9 pad_maximum_fusion
  9.3 8.6 %all-to-all-start = ((bf16[16,160,128]{2,1,0:T(8,128)(2,1)}), bf16[16,160,128]{2,1,0:T(8,128)(2,1)S(1)}, u32[]{:S(2)}, u32[]{:S(2)}) async-start(bf16[16,160,128]{2,1,0:T(8,128)(2,1)} %pad_maximum_fusion), calls=%async_computation | async-start | bytes 1310720 | tf_op jit(solution)/shard_map/all_to_all | solution.py:164
  17.9 0.6 fusion.6
  19.7 1.3 pad_add_fusion.info
  21.0 18.4 %all-to-all-done = bf16[16,160,128]{2,1,0:T(8,128)(2,1)S(1)} async-done(((bf16[16,160,128]{2,1,0:T(8,128)(2,1)}), bf16[16,160,128]{2,1,0:T(8,128)(2,1)S(1)}, u32[]{:S(2)}, u32[]{:S(2)}) %all-to-all-start) | async-done | bytes 655392 | tf_op jit(solution)/shard_map/all_to_all | solution.py:164
  39.4 25.4 %all-gather.3.cloned.1.call-done = bf16[1,2560,1024]{2,1,0:T(8,128)(2,1)} async-done(((bf16[1,160,1024]{2,1,0:T(8,128)(2,1)}), bf16[1,2560,1024]{2,1,0:T(8,128)(2,1)}) %all-gather.3.cloned.1.call-update) | async-done | bytes 5242896 | tf_op jit(solution)/shard_map/all_gather | solution.py:161
  64.8 0.0 copy-done
  64.8 24.8 %forward.1 = (bf16[2560,128]{1,0:T(8,128)(2,1)}, bf16[2560,128]{1,0:T(8,128)(2,1)}, bf16[2560,128]{1,0:T(8,128)(2,1)}, bf16[128,2560]{1,0:T(8,128)(2,1)}, bf16[1...) custom-call(s32[4]{0:T(128)} %pad_add_fusion.info, ...), custom_call_target="tpu_custom_call" | custom-call | tf_op jit(solution)/shard_map/forward/pallas_call | solution.py:172
  89.6 0.2 collective-permute-start
  89.8 1.2 collective-permute-done
  91.0 1.0 add_multiply_fusion.2
  92.1 0.8 collective-permute-start.1
  92.8 3.3 %collective-permute-done.1 = f32[4,2560]{1,0:T(4,128)S(1)} collective-permute-done((f32[4,2560]{1,0:T(4,128)S(1)}, f32[4,2560]{1,0:T(4,128)S(1)}, u32[]{:S(2)}, u32[]{:S(2)}) %collective-permute-start.1) | collective-permute-done | bytes 40992 | tf_op jit(solution)/shard_map/ppermute | solution.py:195
  96.2 0.1 add_multiply_fusion.1
  96.3 1.7 %collective-permute-start.2 = (f32[4,2560]{1,0:T(4,128)S(1)}, f32[4,2560]{1,0:T(4,128)S(1)}, u32[]{:S(2)}, u32[]{:S(2)}) collective-permute-start(f32[4,2560]{1,0:T(4,128)S(1)} %pad_maximum_fusion.2), channel_id=1, source_target_pairs={{0,64},{16,80},{32,96},{48,112},{64,0},{80,16},{96,32},{112,48},{1... | collective-permute-start | bytes 122888 | tf_op jit(solution)/shard_map/ppermute | solution.py:195
  98.0 3.7 %collective-permute-done.2 = f32[4,2560]{1,0:T(4,128)S(1)} collective-permute-done((f32[4,2560]{1,0:T(4,128)S(1)}, f32[4,2560]{1,0:T(4,128)S(1)}, u32[]{:S(2)}, u32[]{:S(2)}) %collective-permute-start.2) | collective-permute-done | bytes 40992 | tf_op jit(solution)/shard_map/ppermute | solution.py:195
  101.7 0.1 add_multiply_fusion
  101.8 0.7 pad_maximum_fusion.3.stat_ref
  102.4 19.2 %backward.1 = bf16[128,1024]{1,0:T(8,128)(2,1)} custom-call(s32[4]{0:T(128)} %pad_add_fusion.info, bf16[2560,1024]{1,0:T(8,128)(2,1)} %bitcast.14, bf16[2560,128]{1,0:T(8,128)(2,1)} %get-tuple-element.14.q_ref, bf16[2560,128]{1,0:T(8,128)(2,1)} %get-tuple-element.15.k_ref, bf16[2560,128]{1,0:T(8,128)(2,1)} %get-tuple-element.16.v_ref, ...), custom_call_target="tpu_custom_call" | custom-call | tf_op jit(solution)/shard_map/backward/pallas_call | solution.py:206
  121.6 19.0 %all_to_all.10 = bf16[16,8,1024]{2,1,0:T(8,128)(2,1)S(1)} all-to-all(bf16[16,8,1024]{2,1,0:T(8,128)(2,1)} %bitcast.18), channel_id=1, replica_groups=mesh['seq'=16,'batch'=16] {'batch'}, dimensions={0} | all-to-all | bytes 524288 | tf_op jit(solution)/shard_map/all_to_all | solution.py:220
  140.6 0.7 convert_reduce_fusion
  (6 shorter events, 0.1 us)
Async XLA Ops:
  6.5 11.3 %copy-start.1 = (s32[1,3]{1,0:T(1,128)S(1)}, s32[1,3]{1,0:T(1,128)}, u32[]{:S(2)}) copy-start(s32[1,3]{1,0:T(1,128)} %param.11) | copy-start | bytes 40
  6.5 58.3 %all-gather.3.cloned.1.call-start = ((), (), s32[]{:S(2)}) async-start(), calls=%async_computation.2 | async-start | bytes 5570560 | tf_op jit(solution)/shard_map/all_gather | solution.py:161
  9.3 30.1 %all-to-all-start = ((bf16[16,160,128]{2,1,0:T(8,128)(2,1)}), bf16[16,160,128]{2,1,0:T(8,128)(2,1)S(1)}, u32[]{:S(2)}, u32[]{:S(2)}) async-start(bf16[16,160,128]{2,1,0:T(8,128)(2,1)} %pad_maximum_fusion), calls=%async_computation | async-start | bytes 1310720 | tf_op jit(solution)/shard_map/all_to_all | solution.py:164
  39.4 25.4 %copy-start = (bf16[16,160,128]{2,1,0:T(8,128)(2,1)}, bf16[16,160,128]{2,1,0:T(8,128)(2,1)S(1)}, u32[]{:S(2)}) copy-start(bf16[16,160,128]{2,1,0:T(8,128)(2,1)S(1)} %all-to-all-done) | copy-start | bytes 1966084
  89.6 1.4 collective-permute-start
  92.1 4.1 %collective-permute-start.1 = (f32[4,2560]{1,0:T(4,128)S(1)}, f32[4,2560]{1,0:T(4,128)S(1)}, u32[]{:S(2)}, u32[]{:S(2)}) collective-permute-start(f32[4,2560]{1,0:T(4,128)S(1)} %pad_maximum_fusion.1), channel_id=1, source_target_pairs={{0,32},{16,48},{32,0},{48,16},{64,96},{80,112},{96,64},{112,80},{1... | collective-permute-start | bytes 122888 | tf_op jit(solution)/shard_map/ppermute | solution.py:195
  96.3 5.4 %collective-permute-start.2 = (f32[4,2560]{1,0:T(4,128)S(1)}, f32[4,2560]{1,0:T(4,128)S(1)}, u32[]{:S(2)}, u32[]{:S(2)}) collective-permute-start(f32[4,2560]{1,0:T(4,128)S(1)} %pad_maximum_fusion.2), channel_id=1, source_target_pairs={{0,64},{16,80},{32,96},{48,112},{64,0},{80,16},{96,32},{112,48},{1... | collective-permute-start | bytes 122888 | tf_op jit(solution)/shard_map/ppermute | solution.py:195
Sparse Core Ops, SparseCore 0:
  9.2 55.5 all-gather.2

commit v2 on v1

v2 whole, which is shorter than its diff:
```python
import functools
import jax
import jax.numpy as jnp
from jax import lax
from jax.experimental import pallas as pl
from jax.experimental.pallas import tpu as pltpu
from jax.sharding import PartitionSpec as P

HEADS = 8
BLK = 256
UNROLL = 4
WIDE = 512
F32 = jnp.float32
BF16 = jnp.bfloat16
VMEM_LIMIT = 46 * 1024 * 1024


def nn(a, b):
    return lax.dot_general(a, b, (((1,), (0,)), ((), ())), preferred_element_type=F32)


def nt(a, b):
    return lax.dot_general(a, b, (((1,), (1,)), ((), ())), preferred_element_type=F32)


def silu(z):
    half = 0.5 * z
    return half + half * jnp.tanh(half)


def silu_grad(z):
    half = 0.5 * z
    t = jnp.tanh(half)
    return 0.5 * (1.0 + t) * (1.0 + half * (1.0 - t))


def begin_of(pos, second, third):
    return jnp.where(pos >= third, third, jnp.where(pos >= second, second, 0))


def plan_tiles(blocks, second, third):
    i = jnp.arange(blocks, dtype=jnp.int32)[:, None]
    j = jnp.arange(blocks, dtype=jnp.int32)[None, :]
    low = begin_of(i * BLK, second, third) // BLK
    clear = (begin_of(i * BLK + BLK - 1, second, third) + BLK - 1) // BLK
    used = (j >= low) & (j <= i)
    plain = (used & (j >= clear) & (j < i)).reshape(-1)
    edge = used.reshape(-1) & ~plain
    n_plain = jnp.sum(plain.astype(jnp.int32))
    n_all = n_plain + jnp.sum(edge.astype(jnp.int32))
    place = jnp.where(plain, jnp.cumsum(plain) - 1, jnp.where(edge, n_plain + jnp.cumsum(edge) - 1, -1))
    code = (i * blocks + j).reshape(-1)
    slot = jnp.arange(blocks * blocks + UNROLL, dtype=jnp.int32)
    table = jnp.sum(jnp.where(slot[:, None] == place[None, :], code[None, :], 0), axis=1)
    table = jnp.where(slot < n_all, table, blocks - 1)
    return table.astype(jnp.int32), n_plain, n_all


def block(index):
    return pl.ds(pl.multiple_of(index * BLK, BLK), BLK)


def tile_mask(i, j, second, third, query_rows):
    q_dim, shape = (0, (BLK, 128)) if query_rows else (1, (1, BLK))
    query = i * BLK + lax.broadcasted_iota(jnp.int32, shape, q_dim)
    begin = begin_of(query, second, third)
    if query_rows:
        parts = []
        for at in range(0, BLK, 128):
            key = j * BLK + at + lax.broadcasted_iota(jnp.int32, (BLK, 128), 1)
            parts.append((key <= query) & (key >= begin))
        return parts
    key = j * BLK + lax.broadcasted_iota(jnp.int32, (BLK, BLK), 0)
    return (key <= query) & (key >= begin)


def keep(values, mask):
    if isinstance(mask, list):
        cols = [jnp.where(m, values[:, n * 128:(n + 1) * 128], 0.0) for n, m in enumerate(mask)]
        return jnp.concatenate(cols, axis=1)
    return jnp.where(mask, values, 0.0)


def run_tiles(table, n_plain, n_all, blocks, begin_tile, end_tile):
    def entry(t):
        code = table[t]
        i = code // blocks
        return i, code - i * blocks

    def group(masked):
        def f(u, carry):
            tiles = [entry(u * UNROLL + n) for n in range(UNROLL)]
            state = begin_tile(*tiles[0])
            for n, tile in enumerate(tiles):
                following = begin_tile(*tiles[n + 1]) if n + 1 < UNROLL else None
                end_tile(*tile, state, masked)
                state = following
            return carry
        return f

    plain = n_plain // UNROLL
    lax.fori_loop(0, plain, group(False), 0)
    lax.fori_loop(plain, (n_all + UNROLL - 1) // UNROLL, group(True), 0)


def forward_kernel(info, table, feats_hbm, w_ref, cot, q_ref, k_ref, v_ref, pre_ref, g_ref,
                   att_ref, stat_ref, feats, acc, sem, *, scale):
    role, second, third = info[0], info[1], info[2]
    total, dim = q_ref.shape
    blocks = total // BLK
    loads = []
    for i in range(blocks):
        rows = pl.ds(i * BLK, BLK)
        loads.append(pltpu.make_async_copy(feats_hbm.at[rows, :], feats.at[rows, :], sem.at[i]))
        loads[-1].start()
    for i in range(total // WIDE):
        rows = pl.ds(i * WIDE, WIDE)
        for n in range(WIDE // BLK):
            loads[i * (WIDE // BLK) + n].wait()
        pre = nn(feats[rows, :], w_ref[...])
        pre_q, pre_k = pre[:, :dim], pre[:, dim:2 * dim]
        q_ref[rows, :] = silu(pre_q).astype(BF16)
        k_ref[rows, :] = silu(pre_k).astype(BF16)
        v_ref[rows, :] = silu(pre[:, 2 * dim:3 * dim]).astype(BF16)
        pre_ref[rows, :] = jnp.where(role == 0, pre_q, pre_k)
        g_ref[:, rows] = (cot[rows, :].astype(F32) * silu(pre[:, 3 * dim:])).T
    acc[...] = jnp.zeros_like(acc)

    def begin_tile(i, j):
        return nt(q_ref[block(i), :], k_ref[block(j), :])

    def end_tile(i, j, scores, masked):
        half = scores * (0.5 * scale)
        w = half + half * jnp.tanh(half)
        if masked:
            w = keep(w, tile_mask(i, j, second, third, True))
        acc[block(i), :] += nn(w.astype(BF16), v_ref[block(j), :])

    run_tiles(table, info[3], info[4], blocks, begin_tile, end_tile)
    for i in range(blocks):
        rows = pl.ds(i * BLK, BLK)
        att = acc[rows, :].T
        g = g_ref[:, rows]
        att_ref[:, rows] = att
        mean = jnp.mean(att, axis=0, keepdims=True)
        centered = att - mean
        stat_ref[0:1, rows] = mean
        stat_ref[1:2, rows] = jnp.sum(centered * centered, axis=0, keepdims=True)
        stat_ref[2:3, rows] = jnp.sum(g, axis=0, keepdims=True)
        stat_ref[3:4, rows] = jnp.sum(g * centered, axis=0, keepdims=True)


def backward_kernel(info, table, feats_hbm, q_ref, k_ref, v_ref, pre_ref, g_ref, att_ref,
                    stat_ref, out_ref, feats, datt, acc, dpre, sem, *, scale, width):
    role, second, third = info[0], info[1], info[2]
    total = q_ref.shape[0]
    blocks = total // BLK
    load = pltpu.make_async_copy(feats_hbm, feats, sem)
    load.start()
    for i in range(blocks):
        rows = pl.ds(i * BLK, BLK)
        mean = stat_ref[0:1, rows]
        rstd = lax.rsqrt(stat_ref[1:2, rows] / width + 1e-5)
        g_mean = stat_ref[2:3, rows] / width
        gn_mean = stat_ref[3:4, rows] * rstd / width
        normed = (att_ref[:, rows] - mean) * rstd
        d = rstd * (g_ref[:, rows] - g_mean - normed * gn_mean)
        datt[rows, :] = d.T.astype(BF16)
    acc[...] = jnp.zeros_like(acc)

    def d_scores(scores, dw, mask):
        half = scores * (0.5 * scale)
        t = jnp.tanh(half)
        ds = ((0.5 * scale) + (0.5 * scale) * t) * (1.0 + half * (1.0 - t)) * dw
        if mask is not None:
            ds = keep(ds, mask)
        return ds.astype(BF16)

    def query_begin(i, j):
        return (nt(q_ref[block(i), :], k_ref[block(j), :]), nt(datt[block(i), :], v_ref[block(j), :]))

    def query_end(i, j, state, masked):
        ds = d_scores(*state, tile_mask(i, j, second, third, True) if masked else None)
        acc[block(i), :] += nn(ds, k_ref[block(j), :])

    def key_begin(i, j):
        return (nt(k_ref[block(j), :], q_ref[block(i), :]), nt(v_ref[block(j), :], datt[block(i), :]))

    def key_end(i, j, state, masked):
        ds = d_scores(*state, tile_mask(i, j, second, third, False) if masked else None)
        acc[block(j), :] += nn(ds, q_ref[block(i), :])

    pl.when(role == 0)(lambda: run_tiles(table, info[3], info[4], blocks, query_begin, query_end))
    pl.when(role == 1)(lambda: run_tiles(table, info[3], info[4], blocks, key_begin, key_end))
    for i in range(blocks):
        rows = pl.ds(i * BLK, BLK)
        dpre[:, rows] = (acc[rows, :] * silu_grad(pre_ref[rows, :])).T.astype(BF16)
    load.wait()
    out_ref[...] = nn(dpre[...], feats[...]).astype(out_ref.dtype)


def body(features, w_qk, w_value, w_gate, cotangent, lengths):
    inputs = features[0]
    tok, width = inputs.shape
    n_seq = lax.axis_size("seq")
    n_batch = lax.axis_size("batch")
    total = tok * n_seq
    dim = width // HEADS
    scale = dim ** (-0.5)
    blocks = total // BLK
    s = lax.axis_index("seq")
    head, role = s % HEADS, s // HEADS
    feats = lax.all_gather(inputs, "seq", axis=0, tiled=True)
    pieces = jnp.moveaxis(cotangent[0].reshape(tok, HEADS, dim), 1, 0)
    pieces = jnp.concatenate([pieces, pieces], axis=0)
    cot = lax.all_to_all(pieces, "seq", 0, 0).reshape(total, dim)
    second = lengths[0, 0]
    third = second + lengths[0, 1]
    table, n_plain, n_all = plan_tiles(blocks, second, third)
    info = jnp.stack([role, second, third, n_plain, n_all]).astype(jnp.int32)
    columns = lambda w, at: lax.dynamic_slice_in_dim(w, at * dim, dim, 1)
    weights = jnp.concatenate([
        columns(w_qk, head), columns(w_qk, HEADS + head), columns(w_value, head), columns(w_gate, head),
    ], axis=1)

    smem = pl.BlockSpec(memory_space=pltpu.SMEM)
    vmem = pl.BlockSpec(memory_space=pltpu.VMEM)
    hbm = pl.BlockSpec(memory_space=pltpu.HBM)
    row = jax.ShapeDtypeStruct((total, dim), BF16)
    rowf = jax.ShapeDtypeStruct((total, dim), F32)
    colf = jax.ShapeDtypeStruct((dim, total), F32)
    stat = jax.ShapeDtypeStruct((4, total), F32)
    q, k, v, pre, g, att, stats = pl.pallas_call(
        functools.partial(forward_kernel, scale=scale),
        in_specs=[smem, smem, hbm, vmem, vmem],
        out_specs=[vmem] * 7,
        out_shape=[row, row, row, rowf, colf, colf, stat],
        scratch_shapes=[
            pltpu.VMEM((total, width), BF16),
            pltpu.VMEM((total, dim), F32),
            pltpu.SemaphoreType.DMA((blocks,)),
        ],
        compiler_params=pltpu.CompilerParams(vmem_limit_bytes=VMEM_LIMIT),
        name="forward",
    )(info, table, feats, weights, cot)

    count = dim
    for step in (1, 2, 4):
        other = lax.ppermute(stats, "seq", [(a, a ^ step) for a in range(n_seq)])
        delta = stats[0] - other[0]
        stats = jnp.stack([
            0.5 * (stats[0] + other[0]),
            stats[1] + other[1] + delta * delta * (0.5 * count),
            stats[2] + other[2],
            stats[3] + other[3] + 0.5 * delta * (stats[2] - other[2]),
        ])
        count = 2 * count

    part = pl.pallas_call(
        functools.partial(backward_kernel, scale=scale, width=width),
        in_specs=[smem, smem, hbm] + [vmem] * 7,
        out_specs=vmem,
        out_shape=jax.ShapeDtypeStruct((dim, width), BF16),
        scratch_shapes=[
            pltpu.VMEM((total, width), BF16),
            pltpu.VMEM((total, dim), BF16),
            pltpu.VMEM((total, dim), F32),
            pltpu.VMEM((dim, total), BF16),
            pltpu.SemaphoreType.DMA,
        ],
        compiler_params=pltpu.CompilerParams(vmem_limit_bytes=VMEM_LIMIT),
        name="backward",
    )(info, table, feats, q, k, v, pre, g, att, stats)
    parts = lax.all_to_all(part.reshape(n_batch, dim // n_batch, width), "batch", 0, 0)
    return jnp.sum(parts.astype(F32), axis=0)


def solution(mesh):
    return jax.shard_map(
        body,
        mesh=mesh,
        in_specs=(
            P("batch", "seq", None),
            P(),
            P(),
            P(),
            P("batch", "seq", None),
            P("batch", None),
        ),
        out_specs=P(("seq", "batch"), None),
        check_vma=False,
    )
```

time: 147 us -> 120 us (0.82)
  Pallas kernels: 44 us -> 19.1 us
  waiting for transfers between devices: 52.7 us -> 44.9 us
  local copies, waits for them, and re-layouts: 1.67 us -> 6.03 us
  blocking collectives: 19 us -> 17.2 us
    pallas_call x1, Pallas kernels: 24.8 us -> 11.1 us  [body(): pl.pallas_call(functools.partial(forward_kernel, scale=scale), in_specs=[...]
    pallas_call x1, Pallas kernels: 19.2 us -> 7.96 us  [body(): pl.pallas_call(functools.partial(backward_kernel, scale=scale, width=widt...]
    all_to_all x1, waiting for transfers between devices: 18.4 us -> 10.8 us  [body(): cot = lax.all_to_all(pieces, 'seq', 0, 0).reshape(total, dim)]
    dynamic_slice x0 -> x2, local copies, waits for them, and re-layouts: none -> 2.16 us  [body(): columns = lambda w, at: lax.dynamic_slice_in_dim(w, at * dim, dim, 1)]
    all_to_all x1, blocking collectives: 19 us -> 17.2 us  [body(): lax.all_to_all(part.reshape(n_batch, dim // n_batch, width), 'batch', 0, 0)]
  transfers between devices with their start and end apart: 5 -> 5, of which waited for: 5 -> 5; matrix products, arithmetic and copies ran while one was open for 3% -> 8% of each run, Pallas kernels for 0% -> 0%
where the time goes in v2:
time: 120 us
  waiting for transfers between devices  44.9 us (37%)
  Pallas kernels  19.1 us (16%)
  blocking collectives  17.2 us (14%)
  between operations  16.2 us (14%)
  starting transfers between devices  11.4 us (10%)
  local copies, waits for them, and re-layouts  6.03 us (5%)
  other arithmetic  4.92 us (4%)
    all_gather x1, waiting for transfers between devices, body(): feats = lax.all_gather(inputs, 'seq', axis=0, tiled=True)  25.5 us
    all_to_all x1, blocking collectives, body(): lax.all_to_all(part.reshape(n_batch, dim // n_batch, width), 'batch', 0, 0)  17.2 us
    pallas_call x1, Pallas kernels, body(): pl.pallas_call(functools.partial(forward_kernel, scale=scale), in_specs=[...  11.1 us
    all_to_all x1, waiting for transfers between devices, body(): cot = lax.all_to_all(pieces, 'seq', 0, 0).reshape(total, dim)  10.8 us
    all_to_all x1, starting transfers between devices, body(): cot = lax.all_to_all(pieces, 'seq', 0, 0).reshape(total, dim)  8.57 us
    ppermute x3, waiting for transfers between devices, body(): other = lax.ppermute(stats, 'seq', [(a, a ^ step) for a in range(n_seq)])  7.99 us
    pallas_call x1, Pallas kernels, body(): pl.pallas_call(functools.partial(backward_kernel, scale=scale, width=widt...  7.96 us
    ppermute x3, starting transfers between devices, body(): other = lax.ppermute(stats, 'seq', [(a, a ^ step) for a in range(n_seq)])  2.83 us
  transfers between devices with their start and end apart: 5, of which 5 were waited for; matrix products, arithmetic and copies ran while one was open for 8% of the time, Pallas kernels for 0%

profile of v2, /device:TPU:2, one launch (start us, length us, event | category | flops | bytes accessed | tf_op | source)
XLA Modules:
  0.0 119.8 jit_solution(12896065232983131472)
XLA Ops:
  6.5 0.7 all-gather.3.cloned.1.call-update
  7.3 1.0 copy.16
  8.3 0.9 pad_maximum_fusion.1
  9.2 8.6 %all-to-all-start = ((bf16[16,160,128]{2,1,0:T(8,128)(2,1)}), bf16[16,160,128]{2,1,0:T(8,128)(2,1)S(1)}, u32[]{:S(2)}, u32[]{:S(2)}) async-start(bf16[16,160,128]{2,1,0:T(8,128)(2,1)} %pad_maximum_fusion.1), calls=%async_computation | async-start | bytes 1310720 | tf_op jit(solution)/shard_map/all_to_all | solution.py:216
  17.8 0.6 fusion.10
  19.8 0.7 and_select_fusion.1
  21.0 0.8 convert_reduce_fusion.1
  22.3 0.1 reduce-window.17
  24.0 1.3 %stack.40.info = s32[5]{0:T(128)S(1)} concatenate(s32[1]{0:T(128)} %bitcast, s32[1]{0:T(128)} %bitcast.1, s32[1]{0:T(128)} %bitcast.4, s32[1]{0:T(128)} %bitcast.5, s32[1]{0:T(128)} %bitcast.6), dimensions={0} | concatenate | bytes 40 | tf_op jit(solution)/shard_map/stack | solution.py:220
  25.4 0.7 add_reduce_fusion
  26.2 1.1 constant_dynamic-slice_fusion.3
  27.3 1.1 constant_dynamic-slice_fusion
  28.5 10.8 %all-to-all-done = bf16[16,160,128]{2,1,0:T(8,128)(2,1)S(1)} async-done(((bf16[16,160,128]{2,1,0:T(8,128)(2,1)}), bf16[16,160,128]{2,1,0:T(8,128)(2,1)S(1)}, u32[]{:S(2)}, u32[]{:S(2)}) %all-to-all-start) | async-done | bytes 655392 | tf_op jit(solution)/shard_map/all_to_all | solution.py:216
  39.3 25.5 %all-gather.3.cloned.1.call-done = bf16[1,2560,1024]{2,1,0:T(8,128)(2,1)} async-done(((bf16[1,160,1024]{2,1,0:T(8,128)(2,1)}), bf16[1,2560,1024]{2,1,0:T(8,128)(2,1)}) %all-gather.3.cloned.1.call-update) | async-done | bytes 5242896 | tf_op jit(solution)/shard_map/all_gather | solution.py:213
  64.8 11.1 %forward.1 = (bf16[2560,128]{1,0:T(8,128)(2,1)S(1)}, bf16[2560,128]{1,0:T(8,128)(2,1)S(1)}, bf16[2560,128]{1,0:T(8,128)(2,1)S(1)}, f32[2560,128]{1,0:T(8,128)S(1...) custom-call(s32[5]{0:T(128)S(1)} %stack.40.info, s32[104]{0:T(128)S(1)} %compare_select_fusion.table, ...), custom_call_target="tpu_custom_call" | custom-call | tf_op jit(solution)/shard_map/forward/pallas_call | solution.py:233
  75.9 0.3 collective-permute-start
  76.2 1.0 collective-permute-done
  77.3 0.8 collective-permute-start.1
  78.1 3.3 %collective-permute-done.1 = f32[4,2560]{1,0:T(4,128)S(1)} collective-permute-done((f32[4,2560]{1,0:T(4,128)S(1)}, f32[4,2560]{1,0:T(4,128)S(1)}, u32[]{:S(2)}, u32[]{:S(2)}) %collective-permute-start.1) | collective-permute-done | bytes 40992 | tf_op jit(solution)/shard_map/ppermute | solution.py:249
  81.5 1.7 %collective-permute-start.2 = (f32[4,2560]{1,0:T(4,128)S(1)}, f32[4,2560]{1,0:T(4,128)S(1)}, u32[]{:S(2)}, u32[]{:S(2)}) collective-permute-start(f32[4,2560]{1,0:T(4,128)S(1)} %pad_maximum_fusion.3), channel_id=1, source_target_pairs={{0,64},{16,80},{32,96},{48,112},{64,0},{80,16},{96,32},{112,48},{1... | collective-permute-start | bytes 122888 | tf_op jit(solution)/shard_map/ppermute | solution.py:249
  83.3 3.7 %collective-permute-done.2 = f32[4,2560]{1,0:T(4,128)S(1)} collective-permute-done((f32[4,2560]{1,0:T(4,128)S(1)}, f32[4,2560]{1,0:T(4,128)S(1)}, u32[]{:S(2)}, u32[]{:S(2)}) %collective-permute-start.2) | collective-permute-done | bytes 40992 | tf_op jit(solution)/shard_map/ppermute | solution.py:249
  87.1 8.0 %backward.1 = bf16[128,1024]{1,0:T(8,128)(2,1)S(1)} custom-call(s32[5]{0:T(128)S(1)} %stack.40.info, s32[104]{0:T(128)S(1)} %compare_select_fusion.table, bf16[2560,1024]{1,0:T(8,128)(2,1)} %bitcast.19, bf16[2560,128]{1,0:T(8,128)(2,1)S(1)} %get-tuple-element.12.q_ref, bf16[2560,128]{1,0:T(8,128)(2,1)S(1)} %get-tuple-element.13.k_ref, ...), custom_call_target="tpu_custom_call" | custom-call | tf_op jit(solution)/shard_map/backward/pallas_call | solution.py:259
  95.0 17.2 %all_to_all.10 = bf16[16,8,1024]{2,1,0:T(8,128)(2,1)S(1)} all-to-all(bf16[16,8,1024]{2,1,0:T(8,128)(2,1)S(1)} %bitcast.17), channel_id=1, replica_groups=mesh['seq'=16,'batch'=16] {'batch'}, dimensions={0} | all-to-all | bytes 524288 | tf_op jit(solution)/shard_map/all_to_all | solution.py:274
  112.3 0.7 convert_reduce_fusion
  (31 shorter events, 2.0 us)
Async XLA Ops:
  6.5 11.3 %copy-start = (s32[1,3]{1,0:T(1,128)S(1)}, s32[1,3]{1,0:T(1,128)}, u32[]{:S(2)}) copy-start(s32[1,3]{1,0:T(1,128)} %param.11) | copy-start | bytes 40
  6.5 58.2 %all-gather.3.cloned.1.call-start = ((), (), s32[]{:S(2)}) async-start(), calls=%async_computation.2 | async-start | bytes 5570560 | tf_op jit(solution)/shard_map/all_gather | solution.py:213
  9.2 30.1 %all-to-all-start = ((bf16[16,160,128]{2,1,0:T(8,128)(2,1)}), bf16[16,160,128]{2,1,0:T(8,128)(2,1)S(1)}, u32[]{:S(2)}, u32[]{:S(2)}) async-start(bf16[16,160,128]{2,1,0:T(8,128)(2,1)} %pad_maximum_fusion.1), calls=%async_computation | async-start | bytes 1310720 | tf_op jit(solution)/shard_map/all_to_all | solution.py:216
  75.9 1.3 %collective-permute-start = (f32[4,2560]{1,0:T(4,128)S(1)}, f32[4,2560]{1,0:T(4,128)S(1)}, u32[]{:S(2)}, u32[]{:S(2)}) collective-permute-start(f32[4,2560]{1,0:T(4,128)S(1)} %get-tuple-element.18), channel_id=1, source_target_pairs={{0,16},{16,0},{32,48},{48,32},{64,80},{80,64},{96,112},{112,96},{1... | collective-permute-start | bytes 122888 | tf_op jit(solution)/shard_map/ppermute | solution.py:249
  77.3 4.1 %collective-permute-start.1 = (f32[4,2560]{1,0:T(4,128)S(1)}, f32[4,2560]{1,0:T(4,128)S(1)}, u32[]{:S(2)}, u32[]{:S(2)}) collective-permute-start(f32[4,2560]{1,0:T(4,128)S(1)} %pad_maximum_fusion.2), channel_id=1, source_target_pairs={{0,32},{16,48},{32,0},{48,16},{64,96},{80,112},{96,64},{112,80},{1... | collective-permute-start | bytes 122888 | tf_op jit(solution)/shard_map/ppermute | solution.py:249
  81.5 5.4 %collective-permute-start.2 = (f32[4,2560]{1,0:T(4,128)S(1)}, f32[4,2560]{1,0:T(4,128)S(1)}, u32[]{:S(2)}, u32[]{:S(2)}) collective-permute-start(f32[4,2560]{1,0:T(4,128)S(1)} %pad_maximum_fusion.3), channel_id=1, source_target_pairs={{0,64},{16,80},{32,96},{48,112},{64,0},{80,16},{96,32},{112,48},{1... | collective-permute-start | bytes 122888 | tf_op jit(solution)/shard_map/ppermute | solution.py:249
Sparse Core Ops, SparseCore 0:
  9.2 55.5 all-gather.2

commit v3 on v2

--- a/solution.py
+++ b/solution.py
@@ -12,6 +12,7 @@
 WIDE = 512
 F32 = jnp.float32
 BF16 = jnp.bfloat16
+ROLE, SECOND, THIRD, PLAIN, ALL, CHIP, CORE, TABLE = range(8)
 VMEM_LIMIT = 46 * 1024 * 1024
 
 
@@ -38,22 +39,38 @@
     return jnp.where(pos >= third, third, jnp.where(pos >= second, second, 0))
 
 
-def plan_tiles(blocks, second, third):
-    i = jnp.arange(blocks, dtype=jnp.int32)[:, None]
-    j = jnp.arange(blocks, dtype=jnp.int32)[None, :]
-    low = begin_of(i * BLK, second, third) // BLK
-    clear = (begin_of(i * BLK + BLK - 1, second, third) + BLK - 1) // BLK
-    used = (j >= low) & (j <= i)
-    plain = (used & (j >= clear) & (j < i)).reshape(-1)
-    edge = used.reshape(-1) & ~plain
-    n_plain = jnp.sum(plain.astype(jnp.int32))
-    n_all = n_plain + jnp.sum(edge.astype(jnp.int32))
-    place = jnp.where(plain, jnp.cumsum(plain) - 1, jnp.where(edge, n_plain + jnp.cumsum(edge) - 1, -1))
-    code = (i * blocks + j).reshape(-1)
-    slot = jnp.arange(blocks * blocks + UNROLL, dtype=jnp.int32)
-    table = jnp.sum(jnp.where(slot[:, None] == place[None, :], code[None, :], 0), axis=1)
-    table = jnp.where(slot < n_all, table, blocks - 1)
-    return table.astype(jnp.int32), n_plain, n_all
+def write_plan(plan, lengths, blocks):
+    s = lax.axis_index("seq")
+    second = lengths[0, 0]
+    third = second + lengths[0, 1]
+    plan[ROLE] = lax.div(s, HEADS)
+    plan[SECOND] = second
+    plan[THIRD] = third
+    plan[CHIP] = lax.div(s, 2)
+    plan[CORE] = lax.rem(s, 2)
+
+    def emit(i, low, high, n):
+        def put(j, at):
+            plan[TABLE + at] = i * blocks + j
+            return at + 1
+        return lax.fori_loop(low, high, put, n)
+
+    ranges = []
+    for i in range(blocks):
+        low = lax.div(begin_of(i * BLK, second, third), BLK)
+        clear = lax.div(begin_of(i * BLK + BLK - 1, second, third) + BLK - 1, BLK)
+        ranges.append((low, jnp.minimum(jnp.maximum(clear, low), i)))
+    n = jnp.int32(0)
+    for i, (low, clear) in enumerate(ranges):
+        n = emit(i, clear, i, n)
+    plan[PLAIN] = n
+    for i, (low, clear) in enumerate(ranges):
+        n = emit(i, low, clear, n)
+        plan[TABLE + n] = i * blocks + i
+        n = n + 1
+    plan[ALL] = n
+    for pad in range(UNROLL):
+        plan[TABLE + n + pad] = blocks - 1
 
 
 def block(index):
@@ -83,7 +100,7 @@
 
 def run_tiles(table, n_plain, n_all, blocks, begin_tile, end_tile):
     def entry(t):
-        code = table[t]
+        code = table[TABLE + t]
         i = code // blocks
         return i, code - i * blocks
 
@@ -103,20 +120,38 @@
     lax.fori_loop(plain, (n_all + UNROLL - 1) // UNROLL, group(True), 0)
 
 
-def forward_kernel(info, table, feats_hbm, w_ref, cot, q_ref, k_ref, v_ref, pre_ref, g_ref,
-                   att_ref, stat_ref, feats, acc, sem, *, scale):
-    role, second, third = info[0], info[1], info[2]
+def prepare_kernel(lengths, own, wqk_hbm, wv_hbm, wu_hbm, plan, w_ref, feats, sem, own_sem, *, blocks):
+    s = lax.axis_index("seq")
+    dim = w_ref.shape[1] // 4
+    head = lax.rem(s, HEADS) * dim
+    width = wv_hbm.shape[1]
+    tok = own.shape[0]
+    copies = [pltpu.make_async_copy(own, feats.at[pl.ds(pl.multiple_of(s * tok, 16), tok), :], own_sem)]
+    for n, (source, at) in enumerate(((wqk_hbm, head), (wqk_hbm, width + head), (wv_hbm, head), (wu_hbm, head))):
+        columns = pl.ds(pl.multiple_of(at, 128), dim)
+        copies.append(pltpu.make_async_copy(
+            source.at[:, columns], w_ref.at[:, pl.ds(n * dim, dim)], sem.at[n]))
+    for copy in copies:
+        copy.start()
+    write_plan(plan, lengths, blocks)
+    for copy in copies:
+        copy.wait()
+
+
+def forward_kernel(plan, w_ref, cot, feats_hbm, q_ref, k_ref, v_ref, pre_ref, g_ref, att_ref,
+                   stat_ref, feats, acc, sem, *, scale):
+    role, second, third = plan[ROLE], plan[SECOND], plan[THIRD]
     total, dim = q_ref.shape
     blocks = total // BLK
     loads = []
-    for i in range(blocks):
-        rows = pl.ds(i * BLK, BLK)
+    for i in range(total // WIDE):
+        rows = pl.ds(i * WIDE, WIDE)
         loads.append(pltpu.make_async_copy(feats_hbm.at[rows, :], feats.at[rows, :], sem.at[i]))
         loads[-1].start()
+    acc[...] = jnp.zeros_like(acc)
     for i in range(total // WIDE):
         rows = pl.ds(i * WIDE, WIDE)
-        for n in range(WIDE // BLK):
-            loads[i * (WIDE // BLK) + n].wait()
+        loads[i].wait()
         pre = nn(feats[rows, :], w_ref[...])
         pre_q, pre_k = pre[:, :dim], pre[:, dim:2 * dim]
         q_ref[rows, :] = silu(pre_q).astype(BF16)
@@ -124,7 +159,6 @@
         v_ref[rows, :] = silu(pre[:, 2 * dim:3 * dim]).astype(BF16)
         pre_ref[rows, :] = jnp.where(role == 0, pre_q, pre_k)
         g_ref[:, rows] = (cot[rows, :].astype(F32) * silu(pre[:, 3 * dim:])).T
-    acc[...] = jnp.zeros_like(acc)
 
     def begin_tile(i, j):
         return nt(q_ref[block(i), :], k_ref[block(j), :])
@@ -136,7 +170,7 @@
             w = keep(w, tile_mask(i, j, second, third, True))
         acc[block(i), :] += nn(w.astype(BF16), v_ref[block(j), :])
 
-    run_tiles(table, info[3], info[4], blocks, begin_tile, end_tile)
+    run_tiles(plan, plan[PLAIN], plan[ALL], blocks, begin_tile, end_tile)
     for i in range(blocks):
         rows = pl.ds(i * BLK, BLK)
         att = acc[rows, :].T
@@ -150,9 +184,10 @@
         stat_ref[3:4, rows] = jnp.sum(g * centered, axis=0, keepdims=True)
 
 
-def backward_kernel(info, table, feats_hbm, q_ref, k_ref, v_ref, pre_ref, g_ref, att_ref,
-                    stat_ref, out_ref, feats, datt, acc, dpre, sem, *, scale, width):
-    role, second, third = info[0], info[1], info[2]
+def backward_kernel(plan, feats_hbm, q_ref, k_ref, v_ref, pre_ref, g_ref, att_ref, stat_ref,
+                    out_ref, feats, datt, acc, dpre, sem, *, scale, width):
+    table = plan
+    role, second, third = plan[ROLE], plan[SECOND], plan[THIRD]
     total = q_ref.shape[0]
     blocks = total // BLK
     load = pltpu.make_async_copy(feats_hbm, feats, sem)
@@ -190,8 +225,8 @@
         ds = d_scores(*state, tile_mask(i, j, second, third, False) if masked else None)
         acc[block(j), :] += nn(ds, q_ref[block(i), :])
 
-    pl.when(role == 0)(lambda: run_tiles(table, info[3], info[4], blocks, query_begin, query_end))
-    pl.when(role == 1)(lambda: run_tiles(table, info[3], info[4], blocks, key_begin, key_end))
+    pl.when(role == 0)(lambda: run_tiles(table, plan[PLAIN], plan[ALL], blocks, query_begin, query_end))
+    pl.when(role == 1)(lambda: run_tiles(table, plan[PLAIN], plan[ALL], blocks, key_begin, key_end))
     for i in range(blocks):
         rows = pl.ds(i * BLK, BLK)
         dpre[:, rows] = (acc[rows, :] * silu_grad(pre_ref[rows, :])).T.astype(BF16)
@@ -208,41 +243,83 @@
     dim = width // HEADS
     scale = dim ** (-0.5)
     blocks = total // BLK
+    chips = n_seq // 2
+    half = tok // 2
     s = lax.axis_index("seq")
-    head, role = s % HEADS, s // HEADS
-    feats = lax.all_gather(inputs, "seq", axis=0, tiled=True)
-    pieces = jnp.moveaxis(cotangent[0].reshape(tok, HEADS, dim), 1, 0)
-    pieces = jnp.concatenate([pieces, pieces], axis=0)
-    cot = lax.all_to_all(pieces, "seq", 0, 0).reshape(total, dim)
-    second = lengths[0, 0]
-    third = second + lengths[0, 1]
-    table, n_plain, n_all = plan_tiles(blocks, second, third)
-    info = jnp.stack([role, second, third, n_plain, n_all]).astype(jnp.int32)
-    columns = lambda w, at: lax.dynamic_slice_in_dim(w, at * dim, dim, 1)
-    weights = jnp.concatenate([
-        columns(w_qk, head), columns(w_qk, HEADS + head), columns(w_value, head), columns(w_gate, head),
-    ], axis=1)
+    core = s % 2
+
+    def shift(x, by):
+        return lax.ppermute(x, "seq", [(a, (a + 2 * by) % n_seq) for a in range(n_seq)])
+
+    def swap(x):
+        return lax.ppermute(x, "seq", [(a, a ^ 1) for a in range(n_seq)])
+
+    def place(feats, piece, by, other, offset=0):
+        first = ((s // 2 + by) % chips * 2 + (1 - core if other else core)) * tok + offset
+        return lax.dynamic_update_slice(feats, piece, (first, 0))
 
     smem = pl.BlockSpec(memory_space=pltpu.SMEM)
     vmem = pl.BlockSpec(memory_space=pltpu.VMEM)
     hbm = pl.BlockSpec(memory_space=pltpu.HBM)
+    params = pltpu.CompilerParams(vmem_limit_bytes=VMEM_LIMIT)
+
+    plan, weights, feats = pl.pallas_call(
+        functools.partial(prepare_kernel, blocks=blocks),
+        in_specs=[smem] + [hbm] * 4,
+        out_specs=[smem, vmem, hbm],
+        out_shape=[
+            jax.ShapeDtypeStruct((TABLE + blocks * blocks + UNROLL,), jnp.int32),
+            jax.ShapeDtypeStruct((width, 4 * dim), BF16),
+            jax.ShapeDtypeStruct((total, width), BF16),
+        ],
+        scratch_shapes=[pltpu.SemaphoreType.DMA((4,)), pltpu.SemaphoreType.DMA],
+        compiler_params=params,
+        cost_estimate=pl.CostEstimate(flops=0, bytes_accessed=8 * 10 ** 6, transcendentals=0),
+        name="prepare",
+    )(lengths, inputs, w_qk, w_value, w_gate)
+
+    cots = jnp.moveaxis(cotangent[0].reshape(tok, HEADS, dim), 1, 0)
+    cots = jnp.concatenate([cots, cots], axis=0)
+    feats = place(feats, swap(inputs), 0, True)
+    right = left = inputs
+    for step in range(1, chips // 2 + 1):
+        last = step == chips // 2
+        right = shift(right[:half] if last else right, 1)
+        if step > 1:
+            left, feats = lax.optimization_barrier((left, feats))
+        left = shift(left[half:] if last else left, -1)
+        if step == 2:
+            cots, right, left = lax.optimization_barrier((cots, right, left))
+        if step > 1:
+            for piece in pending:
+                feats = place(feats, *piece)
+        if last:
+            right, left, feats = lax.optimization_barrier((right, left, feats))
+            for other in (False, True):
+                feats = place(feats, swap(right) if other else right, step, other)
+                feats = place(feats, swap(left) if other else left, step, other, half)
+        else:
+            pending = [(right, -step, False), (left, step, False), (swap(right), -step, True), (swap(left), step, True)]
+    cot = lax.all_to_all(cots, "seq", 0, 0).reshape(total, dim)
+
     row = jax.ShapeDtypeStruct((total, dim), BF16)
     rowf = jax.ShapeDtypeStruct((total, dim), F32)
     colf = jax.ShapeDtypeStruct((dim, total), F32)
     stat = jax.ShapeDtypeStruct((4, total), F32)
     q, k, v, pre, g, att, stats = pl.pallas_call(
         functools.partial(forward_kernel, scale=scale),
-        in_specs=[smem, smem, hbm, vmem, vmem],
+        in_specs=[smem, vmem, vmem, hbm],
         out_specs=[vmem] * 7,
         out_shape=[row, row, row, rowf, colf, colf, stat],
         scratch_shapes=[
             pltpu.VMEM((total, width), BF16),
             pltpu.VMEM((total, dim), F32),
-            pltpu.SemaphoreType.DMA((blocks,)),
+            pltpu.SemaphoreType.DMA((total // WIDE,)),
         ],
-        compiler_params=pltpu.CompilerParams(vmem_limit_bytes=VMEM_LIMIT),
+        compiler_params=params,
+        cost_estimate=pl.CostEstimate(flops=12 * 10 ** 9, bytes_accessed=12 * 10 ** 6, transcendentals=0),
         name="forward",
-    )(info, table, feats, weights, cot)
+    )(plan, weights, cot, feats)
 
     count = dim
     for step in (1, 2, 4):
@@ -258,7 +335,7 @@
 
     part = pl.pallas_call(
         functools.partial(backward_kernel, scale=scale, width=width),
-        in_specs=[smem, smem, hbm] + [vmem] * 7,
+        in_specs=[smem, hbm] + [vmem] * 7,
         out_specs=vmem,
         out_shape=jax.ShapeDtypeStruct((dim, width), BF16),
         scratch_shapes=[
@@ -268,9 +345,9 @@
             pltpu.VMEM((dim, total), BF16),
             pltpu.SemaphoreType.DMA,
         ],
-        compiler_params=pltpu.CompilerParams(vmem_limit_bytes=VMEM_LIMIT),
+        compiler_params=params,
         name="backward",
-    )(info, table, feats, q, k, v, pre, g, att, stats)
+    )(plan, feats, q, k, v, pre, g, att, stats)
     parts = lax.all_to_all(part.reshape(n_batch, dim // n_batch, width), "batch", 0, 0)
     return jnp.sum(parts.astype(F32), axis=0)
 

time: 120 us -> 111 us (0.925)
  waiting for transfers between devices: 44.9 us -> 27.5 us
  between operations: 16.2 us -> 0.27 us
  local copies, waits for them, and re-layouts: 6.03 us -> 19.4 us
  starting transfers between devices: 11.4 us -> 23.8 us
  Pallas kernels: 19.1 us -> 23.2 us
  blocking collectives: 17.2 us -> 14.1 us
  other arithmetic: 4.92 us -> 1.87 us
    all_gather x1 -> x0, waiting for transfers between devices: 25.5 us -> none  [body(): feats = lax.all_gather(inputs, 'seq', axis=0, tiled=True)]
    ppermute x0 -> x17, waiting for transfers between devices: none -> 18.9 us  [the longest x8 18.9 us: shift(): lax.ppermute(x, 'seq', [(a, (a + 2 * by) % n_seq) for a in range(n_seq)])]
    ppermute x0 -> x17, starting transfers between devices: none -> 17.9 us  [the longest x8 16.3 us: shift(): lax.ppermute(x, 'seq', [(a, (a + 2 * by) % n_seq) for a in range(n_seq)])]
    dynamic_update_slice x0 -> x17, local copies, waits for them, and re-layouts: none -> 13.5 us  [place(): return lax.dynamic_update_slice(feats, piece, (first, 0))]
    all_to_all x1, waiting for transfers between devices: 10.8 us -> 0.01 us  [body(): cot = lax.all_to_all(cots, 'seq', 0, 0).reshape(total, dim)]
    all_to_all x1, starting transfers between devices: 8.57 us -> 3.59 us  [body(): cot = lax.all_to_all(cots, 'seq', 0, 0).reshape(total, dim)]
    unnamed x3 -> x9, local copies, waits for them, and re-layouts: 1.03 us -> 5.83 us
    all_to_all x1, blocking collectives: 17.2 us -> 14.1 us  [body(): lax.all_to_all(part.reshape(n_batch, dim // n_batch, width), 'batch', 0, 0)]
  transfers between devices with their start and end apart: 5 -> 21, of which waited for: 5 -> 9; matrix products, arithmetic and copies ran while one was open for 8% -> 14% of each run, Pallas kernels for 0% -> 2%
where the time goes in v3:
time: 111 us; the launch traced here: 110 us
  waiting for transfers between devices  27.5 us (25%)
  starting transfers between devices  23.8 us (21%)
  Pallas kernels  23.2 us (21%)
  local copies, waits for them, and re-layouts  19.4 us (17%)
  blocking collectives  14.1 us (13%)
  other arithmetic  1.87 us (2%)
    ppermute x8, waiting for transfers between devices, shift(): lax.ppermute(x, 'seq', [(a, (a + 2 * by) % n_seq) for a in range(n_seq)])  18.9 us
    ppermute x8, starting transfers between devices, shift(): lax.ppermute(x, 'seq', [(a, (a + 2 * by) % n_seq) for a in range(n_seq)])  16.3 us
    all_to_all x1, blocking collectives, body(): lax.all_to_all(part.reshape(n_batch, dim // n_batch, width), 'batch', 0, 0)  14.1 us
    dynamic_update_slice x17, local copies, waits for them, and re-layouts, place(): return lax.dynamic_update_slice(feats, piece, (first, 0))  13.5 us
    pallas_call x1, Pallas kernels, body(): pl.pallas_call(functools.partial(forward_kernel, scale=scale), in_specs=[...  11.9 us
    pallas_call x1, Pallas kernels, body(): pl.pallas_call(functools.partial(backward_kernel, scale=scale, width=widt...  8.97 us
    ppermute x3, waiting for transfers between devices, body(): other = lax.ppermute(stats, 'seq', [(a, a ^ step) for a in range(n_seq)])  8.53 us
    unnamed x9, local copies, waits for them, and re-layouts  5.83 us
  transfers between devices with their start and end apart: 21, of which 9 were waited for; matrix products, arithmetic and copies ran while one was open for 14% of the time, Pallas kernels for 2%

profile of v3, /device:TPU:2, one launch (start us, length us, event | category | flops | bytes accessed | tf_op | source)
XLA Modules:
  0.0 110.0 jit_solution(2061506279081255805)
XLA Ops:
  0.0 5.9 %collective-permute-start.2 = (bf16[160,1024]{1,0:T(8,128)(2,1)}, bf16[160,1024]{1,0:T(8,128)(2,1)S(1)}, u32[]{:S(2)}, u32[]{:S(2)}) collective-permute-start(bf16[160,1024]{1,0:T(8,128)(2,1)} %bitcast.12), channel_id=1, source_target_pairs={{0,224},{16,240},{32,0},{48,16},{64,32},{80,48},{96,64},{112,80},{... | collective-permute-start | bytes 983048 | tf_op jit(solution)/shard_map/ppermute | solution.py:252
  5.9 1.0 copy.8
  7.1 1.6 %copy-done = bf16[1024,1024]{1,0:T(8,128)(2,1)S(1)} copy-done((bf16[1024,1024]{1,0:T(8,128)(2,1)S(1)}, bf16[1024,1024]{1,0:T(8,128)(2,1)}, u32[]{:S(2)}) %copy-start) | copy-done | bytes 2097176
  8.7 1.6 %copy-done.1 = bf16[1024,1024]{1,0:T(8,128)(2,1)S(1)} copy-done((bf16[1024,1024]{1,0:T(8,128)(2,1)S(1)}, bf16[1024,1024]{1,0:T(8,128)(2,1)}, u32[]{:S(2)}) %copy-start.1) | copy-done | bytes 2097176
  10.2 1.0 copy-done.2
  11.9 2.3 %prepare.1 = (s32[111]{0:T(128)S(1)}, bf16[1024,512]{1,0:T(8,128)(2,1)S(1)}, bf16[2560,1024]{1,0:T(8,128)(2,1)}) custom-call(s32[1,3]{1,0:T(1,128)S(1)} %copy-done.3, bf16[160,1024]{1,0:T(8,128)(2,1)S(1)} %bitcast.14, bf16[1024,2048]{1,0:T(8,128)(2,1)} %wqk_hbm.1, bf16[1024,1024]{1,0:T(8,128)(2,1)S(1)} %copy-done, bf16[1024,1024]{1,0:T(8,128)(2,1)S(1)} %copy-done.1), custom_call_target="tpu_custom_call" | custom-call | bytes 8000000 | tf_op jit(solution)/shard_map/prepare/pallas_call | solution.py:266
  15.0 3.3 %collective-permute-start.4 = (bf16[160,1024]{1,0:T(8,128)(2,1)S(1)}, bf16[160,1024]{1,0:T(8,128)(2,1)S(1)}, u32[]{:S(2)}, u32[]{:S(2)}) collective-permute-start(bf16[160,1024]{1,0:T(8,128)(2,1)S(1)} %collective-permute-done.2), channel_id=1, source_target_pairs={{0,224},{16,240},{32,0},{48,16},{64,32},{80,48},{96,64},{112,80},{... | collective-permute-start | bytes 983048 | tf_op jit(solution)/shard_map/ppermute | solution.py:252
  18.3 0.9 pad_maximum_fusion
  21.2 4.1 %collective-permute-done.4 = bf16[160,1024]{1,0:T(8,128)(2,1)S(1)} collective-permute-done((bf16[160,1024]{1,0:T(8,128)(2,1)S(1)}, bf16[160,1024]{1,0:T(8,128)(2,1)S(1)}, u32[]{:S(2)}, u32[]{:S(2)}) %collective-permute-start.4) | collective-permute-done | bytes 327712 | tf_op jit(solution)/shard_map/ppermute | solution.py:252
  25.3 4.3 %collective-permute-done.1 = bf16[160,1024]{1,0:T(8,128)(2,1)S(1)} collective-permute-done((bf16[160,1024]{1,0:T(8,128)(2,1)S(1)}, bf16[160,1024]{1,0:T(8,128)(2,1)S(1)}, u32[]{:S(2)}, u32[]{:S(2)}) %collective-permute-start.1) | collective-permute-done | bytes 327712 | tf_op jit(solution)/shard_map/ppermute | solution.py:252
  31.6 2.9 %collective-permute-start.9 = (bf16[160,1024]{1,0:T(8,128)(2,1)S(1)}, bf16[160,1024]{1,0:T(8,128)(2,1)S(1)}, u32[]{:S(2)}, u32[]{:S(2)}) collective-permute-start(bf16[160,1024]{1,0:T(8,128)(2,1)S(1)} %collective-permute-done.4), channel_id=1, source_target_pairs={{0,224},{16,240},{32,0},{48,16},{64,32},{80,48},{96,64},{112,80},{... | collective-permute-start | bytes 983048 | tf_op jit(solution)/shard_map/ppermute | solution.py:252
  34.6 3.6 %all-to-all-start = ((bf16[16,160,128]{2,1,0:T(8,128)(2,1)}), bf16[16,160,128]{2,1,0:T(8,128)(2,1)S(1)}, u32[]{:S(2)}, u32[]{:S(2)}) async-start(bf16[16,160,128]{2,1,0:T(8,128)(2,1)} %pad_maximum_fusion), calls=%async_computation | async-start | bytes 1310720 | tf_op jit(solution)/shard_map/all_to_all | solution.py:303
  39.7 1.2 %collective-permute-done.5 = bf16[160,1024]{1,0:T(8,128)(2,1)S(1)} collective-permute-done((bf16[160,1024]{1,0:T(8,128)(2,1)S(1)}, bf16[160,1024]{1,0:T(8,128)(2,1)S(1)}, u32[]{:S(2)}, u32[]{:S(2)}) %collective-permute-start.5) | collective-permute-done | bytes 327712 | tf_op jit(solution)/shard_map/ppermute | solution.py:252
  41.7 1.8 %constant_dynamic-update-slice_fusion.8 = bf16[2560,1024]{1,0:T(8,128)(2,1)} fusion(bf16[2560,1024]{1,0:T(8,128)(2,1)} %constant_dynamic-update-slice_fusion.9, bf16[160,1024]{1,0:T(8,128)(2,1)} %collective-permute-done.11, s32[]{:T(128)S(6)} %select_n.143), kind=kLoop, calls=%fused_computation.35 | loop fusion | bytes 655364 | tf_op jit(solution)/shard_map/dynamic_update_slice | solution.py:259
  43.4 3.7 %collective-permute-done.9 = bf16[160,1024]{1,0:T(8,128)(2,1)S(1)} collective-permute-done((bf16[160,1024]{1,0:T(8,128)(2,1)S(1)}, bf16[160,1024]{1,0:T(8,128)(2,1)S(1)}, u32[]{:S(2)}, u32[]{:S(2)}) %collective-permute-start.9) | collective-permute-done | bytes 327712 | tf_op jit(solution)/shard_map/ppermute | solution.py:252
  47.2 4.1 %collective-permute-start.12 = (bf16[80,1024]{1,0:T(8,128)(2,1)S(1)}, bf16[80,1024]{1,0:T(8,128)(2,1)S(1)}, u32[]{:S(2)}, u32[]{:S(2)}) collective-permute-start(bf16[80,1024]{1,0:T(8,128)(2,1)S(1)} %slice.63), channel_id=1, source_target_pairs={{0,224},{16,240},{32,0},{48,16},{64,32},{80,48},{96,64},{112,80},{... | collective-permute-start | bytes 491528 | tf_op jit(solution)/shard_map/ppermute | solution.py:252
  54.5 5.0 %collective-permute-done.12 = bf16[80,1024]{1,0:T(8,128)(2,1)S(1)} collective-permute-done((bf16[80,1024]{1,0:T(8,128)(2,1)S(1)}, bf16[80,1024]{1,0:T(8,128)(2,1)S(1)}, u32[]{:S(2)}, u32[]{:S(2)}) %collective-permute-start.12) | collective-permute-done | bytes 163872 | tf_op jit(solution)/shard_map/ppermute | solution.py:252
  63.3 11.9 %forward.1 = (bf16[2560,128]{1,0:T(8,128)(2,1)S(1)}, bf16[2560,128]{1,0:T(8,128)(2,1)S(1)}, bf16[2560,128]{1,0:T(8,128)(2,1)S(1)}, f32[2560,128]{1,0:T(8,128)S(1...) custom-call(s32[111]{0:T(128)S(1)} %get-tuple-element.27.plan, ...), custom_call_target="tpu_custom_call" | custom-call | flops 12000000000 | bytes 12000000 | tf_op jit(solution)/shard_map/forward/pallas_call | solution.py:309
  75.3 1.2 %collective-permute-done.17 = f32[4,2560]{1,0:T(4,128)S(1)} collective-permute-done((f32[4,2560]{1,0:T(4,128)S(1)}, f32[4,2560]{1,0:T(4,128)S(1)}, u32[]{:S(2)}, u32[]{:S(2)}) %collective-permute-start.17) | collective-permute-done | bytes 40992 | tf_op jit(solution)/shard_map/ppermute | solution.py:326
  76.9 3.8 %collective-permute-done.18 = f32[4,2560]{1,0:T(4,128)S(1)} collective-permute-done((f32[4,2560]{1,0:T(4,128)S(1)}, f32[4,2560]{1,0:T(4,128)S(1)}, u32[]{:S(2)}, u32[]{:S(2)}) %collective-permute-start.18) | collective-permute-done | bytes 40992 | tf_op jit(solution)/shard_map/ppermute | solution.py:326
  80.8 1.9 %collective-permute-start.19 = (f32[4,2560]{1,0:T(4,128)S(1)}, f32[4,2560]{1,0:T(4,128)S(1)}, u32[]{:S(2)}, u32[]{:S(2)}) collective-permute-start(f32[4,2560]{1,0:T(4,128)S(1)} %pad_maximum_fusion.2), channel_id=1, source_target_pairs={{0,64},{16,80},{32,96},{48,112},{64,0},{80,16},{96,32},{112,48},{1... | collective-permute-start | bytes 122888 | tf_op jit(solution)/shard_map/ppermute | solution.py:326
  82.7 3.6 %collective-permute-done.19 = f32[4,2560]{1,0:T(4,128)S(1)} collective-permute-done((f32[4,2560]{1,0:T(4,128)S(1)}, f32[4,2560]{1,0:T(4,128)S(1)}, u32[]{:S(2)}, u32[]{:S(2)}) %collective-permute-start.19) | collective-permute-done | bytes 40992 | tf_op jit(solution)/shard_map/ppermute | solution.py:326
  86.3 9.0 %backward.1 = bf16[128,1024]{1,0:T(8,128)(2,1)S(1)} custom-call(s32[111]{0:T(128)S(1)} %get-tuple-element.27.plan, bf16[2560,1024]{1,0:T(8,128)(2,1)} %constant_dynamic-update-slice_fusion.feats_hbm, bf16[2560,128]{1,0:T(8,128)(2,1)S(1)} %get-tuple-element.42.q_ref, bf16[2560,128]{1,0:T(8,128)(2,1)S(1)} %get-tuple-element.43.k_ref, ...), custom_call_target="tpu_custom_call" | custom-call | tf_op jit(solution)/shard_map/backward/pallas_call | solution.py:336
  95.3 14.1 %all_to_all.10 = bf16[16,8,1024]{2,1,0:T(8,128)(2,1)S(1)} all-to-all(bf16[16,8,1024]{2,1,0:T(8,128)(2,1)S(1)} %bitcast.9), channel_id=1, replica_groups=mesh['seq'=16,'batch'=16] {'batch'}, dimensions={0} | all-to-all | bytes 524288 | tf_op jit(solution)/shard_map/all_to_all | solution.py:351
  (59 shorter events, 16.1 us)
Async XLA Ops:
  0.0 14.2 %collective-permute-start.3 = (bf16[160,1024]{1,0:T(8,128)(2,1)}, bf16[160,1024]{1,0:T(8,128)(2,1)S(1)}, u32[]{:S(2)}, u32[]{:S(2)}) collective-permute-start(bf16[160,1024]{1,0:T(8,128)(2,1)} %bitcast.11), channel_id=1, source_target_pairs={{0,16},{16,0},{32,48},{48,32},{64,80},{80,64},{96,112},{112,96},{1... | collective-permute-start | bytes 983048 | tf_op jit(solution)/shard_map/ppermute | solution.py:255
  0.0 15.0 %collective-permute-start.2 = (bf16[160,1024]{1,0:T(8,128)(2,1)}, bf16[160,1024]{1,0:T(8,128)(2,1)S(1)}, u32[]{:S(2)}, u32[]{:S(2)}) collective-permute-start(bf16[160,1024]{1,0:T(8,128)(2,1)} %bitcast.12), channel_id=1, source_target_pairs={{0,224},{16,240},{32,0},{48,16},{64,32},{80,48},{96,64},{112,80},{... | collective-permute-start | bytes 983048 | tf_op jit(solution)/shard_map/ppermute | solution.py:252
  5.9 12.4 %collective-permute-start = (bf16[160,1024]{1,0:T(8,128)(2,1)}, bf16[160,1024]{1,0:T(8,128)(2,1)S(1)}, u32[]{:S(2)}, u32[]{:S(2)}) collective-permute-start(bf16[160,1024]{1,0:T(8,128)(2,1)} %bitcast.13), channel_id=1, source_target_pairs={{0,32},{16,48},{32,64},{48,80},{64,96},{80,112},{96,128},{112,144}... | collective-permute-start | bytes 983048 | tf_op jit(solution)/shard_map/ppermute | solution.py:252
  7.1 1.6 %copy-start = (bf16[1024,1024]{1,0:T(8,128)(2,1)S(1)}, bf16[1024,1024]{1,0:T(8,128)(2,1)}, u32[]{:S(2)}) copy-start(bf16[1024,1024]{1,0:T(8,128)(2,1)} %wv_hbm.1) | copy-start | bytes 6291460
  8.7 1.6 %copy-start.1 = (bf16[1024,1024]{1,0:T(8,128)(2,1)S(1)}, bf16[1024,1024]{1,0:T(8,128)(2,1)}, u32[]{:S(2)}) copy-start(bf16[1024,1024]{1,0:T(8,128)(2,1)} %wu_hbm.1) | copy-start | bytes 6291460
  10.2 1.0 copy-start.2
  15.0 10.3 %collective-permute-start.4 = (bf16[160,1024]{1,0:T(8,128)(2,1)S(1)}, bf16[160,1024]{1,0:T(8,128)(2,1)S(1)}, u32[]{:S(2)}, u32[]{:S(2)}) collective-permute-start(bf16[160,1024]{1,0:T(8,128)(2,1)S(1)} %collective-permute-done.2), channel_id=1, source_target_pairs={{0,224},{16,240},{32,0},{48,16},{64,32},{80,48},{96,64},{112,80},{... | collective-permute-start | bytes 983048 | tf_op jit(solution)/shard_map/ppermute | solution.py:252
  18.2 11.9 %collective-permute-start.7 = (bf16[160,1024]{1,0:T(8,128)(2,1)S(1)}, bf16[160,1024]{1,0:T(8,128)(2,1)S(1)}, u32[]{:S(2)}, u32[]{:S(2)}) collective-permute-start(bf16[160,1024]{1,0:T(8,128)(2,1)S(1)} %collective-permute-done), channel_id=1, source_target_pairs={{0,16},{16,0},{32,48},{48,32},{64,80},{80,64},{96,112},{112,96},{1... | collective-permute-start | bytes 983048 | tf_op jit(solution)/shard_map/ppermute | solution.py:255
  18.2 11.3 %collective-permute-start.1 = (bf16[160,1024]{1,0:T(8,128)(2,1)S(1)}, bf16[160,1024]{1,0:T(8,128)(2,1)S(1)}, u32[]{:S(2)}, u32[]{:S(2)}) collective-permute-start(bf16[160,1024]{1,0:T(8,128)(2,1)S(1)} %collective-permute-done), channel_id=1, source_target_pairs={{0,32},{16,48},{32,64},{48,80},{64,96},{80,112},{96,128},{112,144}... | collective-permute-start | bytes 983048 | tf_op jit(solution)/shard_map/ppermute | solution.py:252
  19.2 11.7 %collective-permute-start.8 = (bf16[160,1024]{1,0:T(8,128)(2,1)S(1)}, bf16[160,1024]{1,0:T(8,128)(2,1)S(1)}, u32[]{:S(2)}, u32[]{:S(2)}) collective-permute-start(bf16[160,1024]{1,0:T(8,128)(2,1)S(1)} %collective-permute-done.2), channel_id=1, source_target_pairs={{0,16},{16,0},{32,48},{48,32},{64,80},{80,64},{96,112},{112,96},{1... | collective-permute-start | bytes 983048 | tf_op jit(solution)/shard_map/ppermute | solution.py:255
  29.6 11.3 %collective-permute-start.10 = (bf16[160,1024]{1,0:T(8,128)(2,1)S(1)}, bf16[160,1024]{1,0:T(8,128)(2,1)S(1)}, u32[]{:S(2)}, u32[]{:S(2)}) collective-permute-start(bf16[160,1024]{1,0:T(8,128)(2,1)S(1)} %collective-permute-done.1), channel_id=1, source_target_pairs={{0,16},{16,0},{32,48},{48,32},{64,80},{80,64},{96,112},{112,96},{1... | collective-permute-start | bytes 983048 | tf_op jit(solution)/shard_map/ppermute | solution.py:255
  29.6 11.3 %collective-permute-start.5 = (bf16[160,1024]{1,0:T(8,128)(2,1)S(1)}, bf16[160,1024]{1,0:T(8,128)(2,1)S(1)}, u32[]{:S(2)}, u32[]{:S(2)}) collective-permute-start(bf16[160,1024]{1,0:T(8,128)(2,1)S(1)} %collective-permute-done.1), channel_id=1, source_target_pairs={{0,32},{16,48},{32,64},{48,80},{64,96},{80,112},{96,128},{112,144}... | collective-permute-start | bytes 983048 | tf_op jit(solution)/shard_map/ppermute | solution.py:252
  29.6 12.1 %collective-permute-start.11 = (bf16[160,1024]{1,0:T(8,128)(2,1)S(1)}, bf16[160,1024]{1,0:T(8,128)(2,1)}, u32[]{:S(2)}, u32[]{:S(2)}) collective-permute-start(bf16[160,1024]{1,0:T(8,128)(2,1)S(1)} %collective-permute-done.4), channel_id=1, source_target_pairs={{0,16},{16,0},{32,48},{48,32},{64,80},{80,64},{96,112},{112,96},{1... | collective-permute-start | bytes 983048 | tf_op jit(solution)/shard_map/ppermute | solution.py:255
  31.6 15.5 %collective-permute-start.9 = (bf16[160,1024]{1,0:T(8,128)(2,1)S(1)}, bf16[160,1024]{1,0:T(8,128)(2,1)S(1)}, u32[]{:S(2)}, u32[]{:S(2)}) collective-permute-start(bf16[160,1024]{1,0:T(8,128)(2,1)S(1)} %collective-permute-done.4), channel_id=1, source_target_pairs={{0,224},{16,240},{32,0},{48,16},{64,32},{80,48},{96,64},{112,80},{... | collective-permute-start | bytes 983048 | tf_op jit(solution)/shard_map/ppermute | solution.py:252
  34.6 28.7 %all-to-all-start = ((bf16[16,160,128]{2,1,0:T(8,128)(2,1)}), bf16[16,160,128]{2,1,0:T(8,128)(2,1)S(1)}, u32[]{:S(2)}, u32[]{:S(2)}) async-start(bf16[16,160,128]{2,1,0:T(8,128)(2,1)} %pad_maximum_fusion), calls=%async_computation | async-start | bytes 1310720 | tf_op jit(solution)/shard_map/all_to_all | solution.py:303
  40.9 12.1 %collective-permute-start.13 = (bf16[160,1024]{1,0:T(8,128)(2,1)S(1)}, bf16[160,1024]{1,0:T(8,128)(2,1)S(1)}, u32[]{:S(2)}, u32[]{:S(2)}) collective-permute-start(bf16[160,1024]{1,0:T(8,128)(2,1)S(1)} %collective-permute-done.5), channel_id=1, source_target_pairs={{0,16},{16,0},{32,48},{48,32},{64,80},{80,64},{96,112},{112,96},{1... | collective-permute-start | bytes 983048 | tf_op jit(solution)/shard_map/ppermute | solution.py:255
  47.2 12.4 %collective-permute-start.12 = (bf16[80,1024]{1,0:T(8,128)(2,1)S(1)}, bf16[80,1024]{1,0:T(8,128)(2,1)S(1)}, u32[]{:S(2)}, u32[]{:S(2)}) collective-permute-start(bf16[80,1024]{1,0:T(8,128)(2,1)S(1)} %slice.63), channel_id=1, source_target_pairs={{0,224},{16,240},{32,0},{48,16},{64,32},{80,48},{96,64},{112,80},{... | collective-permute-start | bytes 491528 | tf_op jit(solution)/shard_map/ppermute | solution.py:252
  51.3 8.7 %collective-permute-start.6 = (bf16[80,1024]{1,0:T(8,128)(2,1)S(1)}, bf16[80,1024]{1,0:T(8,128)(2,1)S(1)}, u32[]{:S(2)}, u32[]{:S(2)}) collective-permute-start(bf16[80,1024]{1,0:T(8,128)(2,1)S(1)} %slice.80), channel_id=1, source_target_pairs={{0,32},{16,48},{32,64},{48,80},{64,96},{80,112},{96,128},{112,144}... | collective-permute-start | bytes 491528 | tf_op jit(solution)/shard_map/ppermute | solution.py:252
  51.4 2.3 %collective-permute-start.14 = (bf16[160,1024]{1,0:T(8,128)(2,1)S(1)}, bf16[160,1024]{1,0:T(8,128)(2,1)S(1)}, u32[]{:S(2)}, u32[]{:S(2)}) collective-permute-start(bf16[160,1024]{1,0:T(8,128)(2,1)S(1)} %collective-permute-done.9), channel_id=1, source_target_pairs={{0,16},{16,0},{32,48},{48,32},{64,80},{80,64},{96,112},{112,96},{1... | collective-permute-start | bytes 983048 | tf_op jit(solution)/shard_map/ppermute | solution.py:255
  60.0 1.9 %collective-permute-start.15 = (bf16[80,1024]{1,0:T(8,128)(2,1)S(1)}, bf16[80,1024]{1,0:T(8,128)(2,1)S(1)}, u32[]{:S(2)}, u32[]{:S(2)}) collective-permute-start(bf16[80,1024]{1,0:T(8,128)(2,1)S(1)} %collective-permute-done.6), channel_id=1, source_target_pairs={{0,16},{16,0},{32,48},{48,32},{64,80},{80,64},{96,112},{112,96},{1... | collective-permute-start | bytes 491528 | tf_op jit(solution)/shard_map/ppermute | solution.py:255
  60.0 2.6 %collective-permute-start.16 = (bf16[80,1024]{1,0:T(8,128)(2,1)S(1)}, bf16[80,1024]{1,0:T(8,128)(2,1)S(1)}, u32[]{:S(2)}, u32[]{:S(2)}) collective-permute-start(bf16[80,1024]{1,0:T(8,128)(2,1)S(1)} %collective-permute-done.12), channel_id=1, source_target_pairs={{0,16},{16,0},{32,48},{48,32},{64,80},{80,64},{96,112},{112,96},{1... | collective-permute-start | bytes 491528 | tf_op jit(solution)/shard_map/ppermute | solution.py:255
  75.2 1.3 %collective-permute-start.17 = (f32[4,2560]{1,0:T(4,128)S(1)}, f32[4,2560]{1,0:T(4,128)S(1)}, u32[]{:S(2)}, u32[]{:S(2)}) collective-permute-start(f32[4,2560]{1,0:T(4,128)S(1)} %get-tuple-element.48), channel_id=1, source_target_pairs={{0,16},{16,0},{32,48},{48,32},{64,80},{80,64},{96,112},{112,96},{1... | collective-permute-start | bytes 122888 | tf_op jit(solution)/shard_map/ppermute | solution.py:326
  76.6 4.1 %collective-permute-start.18 = (f32[4,2560]{1,0:T(4,128)S(1)}, f32[4,2560]{1,0:T(4,128)S(1)}, u32[]{:S(2)}, u32[]{:S(2)}) collective-permute-start(f32[4,2560]{1,0:T(4,128)S(1)} %pad_maximum_fusion.1), channel_id=1, source_target_pairs={{0,32},{16,48},{32,0},{48,16},{64,96},{80,112},{96,64},{112,80},{1... | collective-permute-start | bytes 122888 | tf_op jit(solution)/shard_map/ppermute | solution.py:326
  80.8 5.4 %collective-permute-start.19 = (f32[4,2560]{1,0:T(4,128)S(1)}, f32[4,2560]{1,0:T(4,128)S(1)}, u32[]{:S(2)}, u32[]{:S(2)}) collective-permute-start(f32[4,2560]{1,0:T(4,128)S(1)} %pad_maximum_fusion.2), channel_id=1, source_target_pairs={{0,64},{16,80},{32,96},{48,112},{64,0},{80,16},{96,32},{112,48},{1... | collective-permute-start | bytes 122888 | tf_op jit(solution)/shard_map/ppermute | solution.py:326
  (1 other events, 0.7 us)

commit v4 on v3

--- a/solution.py
+++ b/solution.py
@@ -254,9 +254,10 @@
     def swap(x):
         return lax.ppermute(x, "seq", [(a, a ^ 1) for a in range(n_seq)])
 
-    def place(feats, piece, by, other, offset=0):
-        first = ((s // 2 + by) % chips * 2 + (1 - core if other else core)) * tok + offset
-        return lax.dynamic_update_slice(feats, piece, (first, 0))
+    def place(feats, mine, theirs, by):
+        ordered = [jnp.where(core == 0, a, b) for a, b in zip(mine + theirs, theirs + mine)]
+        first = (s // 2 + by) % chips * (2 * tok)
+        return lax.dynamic_update_slice(feats, jnp.concatenate(ordered, axis=0), (first, 0))
 
     smem = pl.BlockSpec(memory_space=pltpu.SMEM)
     vmem = pl.BlockSpec(memory_space=pltpu.VMEM)
@@ -280,7 +281,7 @@
 
     cots = jnp.moveaxis(cotangent[0].reshape(tok, HEADS, dim), 1, 0)
     cots = jnp.concatenate([cots, cots], axis=0)
-    feats = place(feats, swap(inputs), 0, True)
+    feats = lax.dynamic_update_slice(feats, swap(inputs), ((s - core + 1 - core) * tok, 0))
     right = left = inputs
     for step in range(1, chips // 2 + 1):
         last = step == chips // 2
@@ -295,11 +296,9 @@
                 feats = place(feats, *piece)
         if last:
             right, left, feats = lax.optimization_barrier((right, left, feats))
-            for other in (False, True):
-                feats = place(feats, swap(right) if other else right, step, other)
-                feats = place(feats, swap(left) if other else left, step, other, half)
+            feats = place(feats, (right, left), (swap(right), swap(left)), step)
         else:
-            pending = [(right, -step, False), (left, step, False), (swap(right), -step, True), (swap(left), step, True)]
+            pending = [((right,), (swap(right),), -step), ((left,), (swap(left),), step)]
     cot = lax.all_to_all(cots, "seq", 0, 0).reshape(total, dim)
 
     row = jax.ShapeDtypeStruct((total, dim), BF16)
@@ -322,15 +321,13 @@
     )(plan, weights, cot, feats)
 
     count = dim
+    which = lax.broadcasted_iota(jnp.int32, (4, 1), 0)
     for step in (1, 2, 4):
         other = lax.ppermute(stats, "seq", [(a, a ^ step) for a in range(n_seq)])
-        delta = stats[0] - other[0]
-        stats = jnp.stack([
-            0.5 * (stats[0] + other[0]),
-            stats[1] + other[1] + delta * delta * (0.5 * count),
-            stats[2] + other[2],
-            stats[3] + other[3] + 0.5 * delta * (stats[2] - other[2]),
-        ])
+        both = stats + other
+        delta = stats[0:1] - other[0:1]
+        cross = jnp.where(which == 1, delta * (0.5 * count), 0.5 * (stats[2:3] - other[2:3]))
+        stats = jnp.where(which == 0, 0.5 * both, jnp.where(which == 2, both, both + delta * cross))
         count = 2 * count
 
     part = pl.pallas_call(

time: 111 us -> 110 us (level)
  local copies, waits for them, and re-layouts: 19.4 us -> 5.7 us
  other arithmetic: 1.87 us -> 9.76 us
  waiting for transfers between devices: 27.5 us -> 29.9 us
  blocking collectives: 14.1 us -> 16.2 us
  Pallas kernels: 23.2 us -> 21.6 us
  starting transfers between devices: 23.8 us -> 25.2 us
    dynamic_update_slice x17 -> x1, local copies, waits for them, and re-layouts: 13.5 us -> 0.76 us  [body(): lax.dynamic_update_slice(feats, swap(inputs), ((s - core + 1 - core) * to...]
    dynamic_update_slice x0 -> x7, other arithmetic: none -> 6.3 us  [place(): lax.dynamic_update_slice(feats, jnp.concatenate(ordered, axis=0), (first,...]
    all_to_all x1, blocking collectives: 14.1 us -> 16.2 us  [body(): lax.all_to_all(part.reshape(n_batch, dim // n_batch, width), 'batch', 0, 0)]
    ppermute x8, waiting for transfers between devices: 18.9 us -> 20.6 us  [shift(): lax.ppermute(x, 'seq', [(a, (a + 2 * by) % n_seq) for a in range(n_seq)])]
    select_n x0 -> x11, other arithmetic: none -> 1.59 us  [the longest x8 1.32 us: place(): jnp.where(core == 0, a, b)]
    unnamed x9 -> x11, local copies, waits for them, and re-layouts: 5.83 us -> 4.87 us
  transfers between devices with their start and end apart: 21 -> 21, of which waited for: 9 -> 9; matrix products, arithmetic and copies ran while one was open for 14% -> 9% of each run, Pallas kernels for 2% -> 2%
where the time goes in v4:
time: 110 us; the launch traced here: 109 us
  waiting for transfers between devices  29.9 us (27%)
  starting transfers between devices  25.2 us (23%)
  Pallas kernels  21.6 us (20%)
  blocking collectives  16.2 us (15%)
  other arithmetic  9.76 us (9%)
  local copies, waits for them, and re-layouts  5.7 us (5%)
    ppermute x8, waiting for transfers between devices, shift(): lax.ppermute(x, 'seq', [(a, (a + 2 * by) % n_seq) for a in range(n_seq)])  20.6 us
    ppermute x8, starting transfers between devices, shift(): lax.ppermute(x, 'seq', [(a, (a + 2 * by) % n_seq) for a in range(n_seq)])  17 us
    all_to_all x1, blocking collectives, body(): lax.all_to_all(part.reshape(n_batch, dim // n_batch, width), 'batch', 0, 0)  16.2 us
    pallas_call x1, Pallas kernels, body(): pl.pallas_call(functools.partial(forward_kernel, scale=scale), in_specs=[...  11.2 us
    ppermute x3, waiting for transfers between devices, body(): other = lax.ppermute(stats, 'seq', [(a, a ^ step) for a in range(n_seq)])  8.2 us
    pallas_call x1, Pallas kernels, body(): pl.pallas_call(functools.partial(backward_kernel, scale=scale, width=widt...  8.06 us
    dynamic_update_slice x7, other arithmetic, place(): lax.dynamic_update_slice(feats, jnp.concatenate(ordered, axis=0), (first,...  6.3 us
    unnamed x11, local copies, waits for them, and re-layouts  4.87 us
  transfers between devices with their start and end apart: 21, of which 9 were waited for; matrix products, arithmetic and copies ran while one was open for 9% of the time, Pallas kernels for 2%

profile of v4, /device:TPU:2, one launch (start us, length us, event | category | flops | bytes accessed | tf_op | source)
XLA Modules:
  0.0 108.6 jit_solution(2405328020115805410)
XLA Ops:
  0.0 5.9 %collective-permute-start.2 = (bf16[160,1024]{1,0:T(8,128)(2,1)}, bf16[160,1024]{1,0:T(8,128)(2,1)S(1)}, u32[]{:S(2)}, u32[]{:S(2)}) collective-permute-start(bf16[160,1024]{1,0:T(8,128)(2,1)} %bitcast.12), channel_id=1, source_target_pairs={{0,224},{16,240},{32,0},{48,16},{64,32},{80,48},{96,64},{112,80},{... | collective-permute-start | bytes 983048 | tf_op jit(solution)/shard_map/ppermute | solution.py:252
  5.9 1.6 %copy-done = bf16[1024,1024]{1,0:T(8,128)(2,1)S(1)} copy-done((bf16[1024,1024]{1,0:T(8,128)(2,1)S(1)}, bf16[1024,1024]{1,0:T(8,128)(2,1)}, u32[]{:S(2)}) %copy-start) | copy-done | bytes 2097176
  7.5 1.6 %copy-done.1 = bf16[1024,1024]{1,0:T(8,128)(2,1)S(1)} copy-done((bf16[1024,1024]{1,0:T(8,128)(2,1)S(1)}, bf16[1024,1024]{1,0:T(8,128)(2,1)}, u32[]{:S(2)}) %copy-start.1) | copy-done | bytes 2097176
  9.0 1.0 copy-done.2
  10.7 2.3 %prepare.1 = (s32[111]{0:T(128)S(1)}, bf16[1024,512]{1,0:T(8,128)(2,1)S(1)}, bf16[2560,1024]{1,0:T(8,128)(2,1)}) custom-call(s32[1,3]{1,0:T(1,128)S(1)} %copy-done.3, bf16[160,1024]{1,0:T(8,128)(2,1)S(1)} %bitcast.14, bf16[1024,2048]{1,0:T(8,128)(2,1)} %wqk_hbm.1, bf16[1024,1024]{1,0:T(8,128)(2,1)S(1)} %copy-done, bf16[1024,1024]{1,0:T(8,128)(2,1)S(1)} %copy-done.1), custom_call_target="tpu_custom_call" | custom-call | bytes 8000000 | tf_op jit(solution)/shard_map/prepare/pallas_call | solution.py:267
  13.8 3.3 %collective-permute-done = bf16[160,1024]{1,0:T(8,128)(2,1)S(1)} collective-permute-done((bf16[160,1024]{1,0:T(8,128)(2,1)}, bf16[160,1024]{1,0:T(8,128)(2,1)S(1)}, u32[]{:S(2)}, u32[]{:S(2)}) %collective-permute-start) | collective-permute-done | bytes 327712 | tf_op jit(solution)/shard_map/ppermute | solution.py:252
  17.1 3.2 %collective-permute-start.4 = (bf16[160,1024]{1,0:T(8,128)(2,1)S(1)}, bf16[160,1024]{1,0:T(8,128)(2,1)S(1)}, u32[]{:S(2)}, u32[]{:S(2)}) collective-permute-start(bf16[160,1024]{1,0:T(8,128)(2,1)S(1)} %collective-permute-done.2), channel_id=1, source_target_pairs={{0,224},{16,240},{32,0},{48,16},{64,32},{80,48},{96,64},{112,80},{... | collective-permute-start | bytes 983048 | tf_op jit(solution)/shard_map/ppermute | solution.py:252
  20.5 0.9 pad_maximum_fusion
  21.9 5.4 %collective-permute-done.1 = bf16[160,1024]{1,0:T(8,128)(2,1)S(1)} collective-permute-done((bf16[160,1024]{1,0:T(8,128)(2,1)S(1)}, bf16[160,1024]{1,0:T(8,128)(2,1)S(1)}, u32[]{:S(2)}, u32[]{:S(2)}) %collective-permute-start.1) | collective-permute-done | bytes 327712 | tf_op jit(solution)/shard_map/ppermute | solution.py:252
  27.4 0.9 maximum_dynamic-update-slice_fusion
  29.3 3.2 %collective-permute-start.9 = (bf16[160,1024]{1,0:T(8,128)(2,1)S(1)}, bf16[160,1024]{1,0:T(8,128)(2,1)S(1)}, u32[]{:S(2)}, u32[]{:S(2)}) collective-permute-start(bf16[160,1024]{1,0:T(8,128)(2,1)S(1)} %collective-permute-done.4), channel_id=1, source_target_pairs={{0,224},{16,240},{32,0},{48,16},{64,32},{80,48},{96,64},{112,80},{... | collective-permute-start | bytes 983048 | tf_op jit(solution)/shard_map/ppermute | solution.py:252
  33.0 3.6 %all-to-all-start = ((bf16[16,160,128]{2,1,0:T(8,128)(2,1)}), bf16[16,160,128]{2,1,0:T(8,128)(2,1)S(1)}, u32[]{:S(2)}, u32[]{:S(2)}) async-start(bf16[16,160,128]{2,1,0:T(8,128)(2,1)} %pad_maximum_fusion), calls=%async_computation | async-start | bytes 1310720 | tf_op jit(solution)/shard_map/all_to_all | solution.py:302
  36.7 1.8 %collective-permute-start.6 = (bf16[80,1024]{1,0:T(8,128)(2,1)S(1)}, bf16[80,1024]{1,0:T(8,128)(2,1)S(1)}, u32[]{:S(2)}, u32[]{:S(2)}) collective-permute-start(bf16[80,1024]{1,0:T(8,128)(2,1)S(1)} %slice.56), channel_id=1, source_target_pairs={{0,32},{16,48},{32,64},{48,80},{64,96},{80,112},{96,128},{112,144}... | collective-permute-start | bytes 491528 | tf_op jit(solution)/shard_map/ppermute | solution.py:252
  40.0 1.0 broadcast_select_fusion.5
  41.0 0.9 maximum_dynamic-update-slice_fusion.3
  41.9 2.8 %collective-permute-start.12 = (bf16[80,1024]{1,0:T(8,128)(2,1)S(1)}, bf16[80,1024]{1,0:T(8,128)(2,1)S(1)}, u32[]{:S(2)}, u32[]{:S(2)}) collective-permute-start(bf16[80,1024]{1,0:T(8,128)(2,1)S(1)} %slice.43), channel_id=1, source_target_pairs={{0,224},{16,240},{32,0},{48,16},{64,32},{80,48},{96,64},{112,80},{... | collective-permute-start | bytes 491528 | tf_op jit(solution)/shard_map/ppermute | solution.py:252
  46.7 11.8 %collective-permute-done.6 = bf16[80,1024]{1,0:T(8,128)(2,1)S(1)} collective-permute-done((bf16[80,1024]{1,0:T(8,128)(2,1)S(1)}, bf16[80,1024]{1,0:T(8,128)(2,1)S(1)}, u32[]{:S(2)}, u32[]{:S(2)}) %collective-permute-start.6) | collective-permute-done | bytes 163872 | tf_op jit(solution)/shard_map/ppermute | solution.py:252
  61.0 11.2 %forward.1 = (bf16[2560,128]{1,0:T(8,128)(2,1)S(1)}, bf16[2560,128]{1,0:T(8,128)(2,1)S(1)}, bf16[2560,128]{1,0:T(8,128)(2,1)S(1)}, f32[2560,128]{1,0:T(8,128)S(1...) custom-call(s32[111]{0:T(128)S(1)} %get-tuple-element.27.plan, ...), custom_call_target="tpu_custom_call" | custom-call | flops 12000000000 | bytes 12000000 | tf_op jit(solution)/shard_map/forward/pallas_call | solution.py:308
  72.6 0.9 collective-permute-done.17
  74.1 3.7 %collective-permute-done.18 = f32[4,2560]{1,0:T(4,128)S(1)} collective-permute-done((f32[4,2560]{1,0:T(4,128)S(1)}, f32[4,2560]{1,0:T(4,128)S(1)}, u32[]{:S(2)}, u32[]{:S(2)}) %collective-permute-start.18) | collective-permute-done | bytes 40992 | tf_op jit(solution)/shard_map/ppermute | solution.py:326
  78.0 1.9 %collective-permute-start.19 = (f32[4,2560]{1,0:T(4,128)S(1)}, f32[4,2560]{1,0:T(4,128)S(1)}, u32[]{:S(2)}, u32[]{:S(2)}) collective-permute-start(f32[4,2560]{1,0:T(4,128)S(1)} %fusion.1), channel_id=1, source_target_pairs={{0,64},{16,80},{32,96},{48,112},{64,0},{80,16},{96,32},{112,48},{1... | collective-permute-start | bytes 122888 | tf_op jit(solution)/shard_map/ppermute | solution.py:326
  79.9 3.5 %collective-permute-done.19 = f32[4,2560]{1,0:T(4,128)S(1)} collective-permute-done((f32[4,2560]{1,0:T(4,128)S(1)}, f32[4,2560]{1,0:T(4,128)S(1)}, u32[]{:S(2)}, u32[]{:S(2)}) %collective-permute-start.19) | collective-permute-done | bytes 40992 | tf_op jit(solution)/shard_map/ppermute | solution.py:326
  83.7 8.1 %backward.1 = bf16[128,1024]{1,0:T(8,128)(2,1)S(1)} custom-call(s32[111]{0:T(128)S(1)} %get-tuple-element.27.plan, bf16[2560,1024]{1,0:T(8,128)(2,1)} %maximum_dynamic-update-slice_fusion.6.feats_hbm, bf16[2560,128]{1,0:T(8,128)(2,1)S(1)} %get-tuple-element.42.q_ref, bf16[2560,128]{1,0:T(8,128)(2,1)S(1)} %get-tuple-element.43.k_ref, ...), custom_call_target="tpu_custom_call" | custom-call | tf_op jit(solution)/shard_map/backward/pallas_call | solution.py:333
  91.7 16.2 %all_to_all.10 = bf16[16,8,1024]{2,1,0:T(8,128)(2,1)S(1)} all-to-all(bf16[16,8,1024]{2,1,0:T(8,128)(2,1)S(1)} %bitcast.9), channel_id=1, replica_groups=mesh['seq'=16,'batch'=16] {'batch'}, dimensions={0} | all-to-all | bytes 524288 | tf_op jit(solution)/shard_map/all_to_all | solution.py:348
  (65 shorter events, 11.5 us)
Async XLA Ops:
  0.0 13.0 %collective-permute-start.3 = (bf16[160,1024]{1,0:T(8,128)(2,1)}, bf16[160,1024]{1,0:T(8,128)(2,1)S(1)}, u32[]{:S(2)}, u32[]{:S(2)}) collective-permute-start(bf16[160,1024]{1,0:T(8,128)(2,1)} %bitcast.11), channel_id=1, source_target_pairs={{0,16},{16,0},{32,48},{48,32},{64,80},{80,64},{96,112},{112,96},{1... | collective-permute-start | bytes 983048 | tf_op jit(solution)/shard_map/ppermute | solution.py:255
  0.0 13.8 %collective-permute-start.2 = (bf16[160,1024]{1,0:T(8,128)(2,1)}, bf16[160,1024]{1,0:T(8,128)(2,1)S(1)}, u32[]{:S(2)}, u32[]{:S(2)}) collective-permute-start(bf16[160,1024]{1,0:T(8,128)(2,1)} %bitcast.12), channel_id=1, source_target_pairs={{0,224},{16,240},{32,0},{48,16},{64,32},{80,48},{96,64},{112,80},{... | collective-permute-start | bytes 983048 | tf_op jit(solution)/shard_map/ppermute | solution.py:252
  5.9 11.3 %collective-permute-start = (bf16[160,1024]{1,0:T(8,128)(2,1)}, bf16[160,1024]{1,0:T(8,128)(2,1)S(1)}, u32[]{:S(2)}, u32[]{:S(2)}) collective-permute-start(bf16[160,1024]{1,0:T(8,128)(2,1)} %bitcast.13), channel_id=1, source_target_pairs={{0,32},{16,48},{32,64},{48,80},{64,96},{80,112},{96,128},{112,144}... | collective-permute-start | bytes 983048 | tf_op jit(solution)/shard_map/ppermute | solution.py:252
  5.9 1.6 %copy-start = (bf16[1024,1024]{1,0:T(8,128)(2,1)S(1)}, bf16[1024,1024]{1,0:T(8,128)(2,1)}, u32[]{:S(2)}) copy-start(bf16[1024,1024]{1,0:T(8,128)(2,1)} %wv_hbm.1) | copy-start | bytes 6291460
  7.5 1.6 %copy-start.1 = (bf16[1024,1024]{1,0:T(8,128)(2,1)S(1)}, bf16[1024,1024]{1,0:T(8,128)(2,1)}, u32[]{:S(2)}) copy-start(bf16[1024,1024]{1,0:T(8,128)(2,1)} %wu_hbm.1) | copy-start | bytes 6291460
  10.7 9.7 %copy-start.4 = (bf16[1,160,1024]{2,1,0:T(8,128)(2,1)S(1)}, bf16[1,160,1024]{2,1,0:T(8,128)(2,1)}, u32[]{:S(2)}) copy-start(bf16[1,160,1024]{2,1,0:T(8,128)(2,1)} %param.10) | copy-start | bytes 983044
  17.1 10.2 %collective-permute-start.1 = (bf16[160,1024]{1,0:T(8,128)(2,1)S(1)}, bf16[160,1024]{1,0:T(8,128)(2,1)S(1)}, u32[]{:S(2)}, u32[]{:S(2)}) collective-permute-start(bf16[160,1024]{1,0:T(8,128)(2,1)S(1)} %collective-permute-done), channel_id=1, source_target_pairs={{0,32},{16,48},{32,64},{48,80},{64,96},{80,112},{96,128},{112,144}... | collective-permute-start | bytes 983048 | tf_op jit(solution)/shard_map/ppermute | solution.py:252
  17.1 10.2 %collective-permute-start.4 = (bf16[160,1024]{1,0:T(8,128)(2,1)S(1)}, bf16[160,1024]{1,0:T(8,128)(2,1)S(1)}, u32[]{:S(2)}, u32[]{:S(2)}) collective-permute-start(bf16[160,1024]{1,0:T(8,128)(2,1)S(1)} %collective-permute-done.2), channel_id=1, source_target_pairs={{0,224},{16,240},{32,0},{48,16},{64,32},{80,48},{96,64},{112,80},{... | collective-permute-start | bytes 983048 | tf_op jit(solution)/shard_map/ppermute | solution.py:252
  20.4 7.0 %collective-permute-start.7 = (bf16[160,1024]{1,0:T(8,128)(2,1)S(1)}, bf16[160,1024]{1,0:T(8,128)(2,1)S(1)}, u32[]{:S(2)}, u32[]{:S(2)}) collective-permute-start(bf16[160,1024]{1,0:T(8,128)(2,1)S(1)} %collective-permute-done), channel_id=1, source_target_pairs={{0,16},{16,0},{32,48},{48,32},{64,80},{80,64},{96,112},{112,96},{1... | collective-permute-start | bytes 983048 | tf_op jit(solution)/shard_map/ppermute | solution.py:255
  21.4 6.9 %collective-permute-start.8 = (bf16[160,1024]{1,0:T(8,128)(2,1)S(1)}, bf16[160,1024]{1,0:T(8,128)(2,1)S(1)}, u32[]{:S(2)}, u32[]{:S(2)}) collective-permute-start(bf16[160,1024]{1,0:T(8,128)(2,1)S(1)} %collective-permute-done.2), channel_id=1, source_target_pairs={{0,16},{16,0},{32,48},{48,32},{64,80},{80,64},{96,112},{112,96},{1... | collective-permute-start | bytes 983048 | tf_op jit(solution)/shard_map/ppermute | solution.py:255
  27.4 9.3 %collective-permute-start.5 = (bf16[160,1024]{1,0:T(8,128)(2,1)S(1)}, bf16[160,1024]{1,0:T(8,128)(2,1)S(1)}, u32[]{:S(2)}, u32[]{:S(2)}) collective-permute-start(bf16[160,1024]{1,0:T(8,128)(2,1)S(1)} %collective-permute-done.1), channel_id=1, source_target_pairs={{0,32},{16,48},{32,64},{48,80},{64,96},{80,112},{96,128},{112,144}... | collective-permute-start | bytes 983048 | tf_op jit(solution)/shard_map/ppermute | solution.py:252
  29.3 9.2 %collective-permute-start.9 = (bf16[160,1024]{1,0:T(8,128)(2,1)S(1)}, bf16[160,1024]{1,0:T(8,128)(2,1)S(1)}, u32[]{:S(2)}, u32[]{:S(2)}) collective-permute-start(bf16[160,1024]{1,0:T(8,128)(2,1)S(1)} %collective-permute-done.4), channel_id=1, source_target_pairs={{0,224},{16,240},{32,0},{48,16},{64,32},{80,48},{96,64},{112,80},{... | collective-permute-start | bytes 983048 | tf_op jit(solution)/shard_map/ppermute | solution.py:252
  32.5 6.5 %collective-permute-start.10 = (bf16[160,1024]{1,0:T(8,128)(2,1)S(1)}, bf16[160,1024]{1,0:T(8,128)(2,1)S(1)}, u32[]{:S(2)}, u32[]{:S(2)}) collective-permute-start(bf16[160,1024]{1,0:T(8,128)(2,1)S(1)} %collective-permute-done.1), channel_id=1, source_target_pairs={{0,16},{16,0},{32,48},{48,32},{64,80},{80,64},{96,112},{112,96},{1... | collective-permute-start | bytes 983048 | tf_op jit(solution)/shard_map/ppermute | solution.py:255
  32.5 7.5 %collective-permute-start.11 = (bf16[160,1024]{1,0:T(8,128)(2,1)S(1)}, bf16[160,1024]{1,0:T(8,128)(2,1)}, u32[]{:S(2)}, u32[]{:S(2)}) collective-permute-start(bf16[160,1024]{1,0:T(8,128)(2,1)S(1)} %collective-permute-done.4), channel_id=1, source_target_pairs={{0,16},{16,0},{32,48},{48,32},{64,80},{80,64},{96,112},{112,96},{1... | collective-permute-start | bytes 983048 | tf_op jit(solution)/shard_map/ppermute | solution.py:255
  33.0 28.0 %all-to-all-start = ((bf16[16,160,128]{2,1,0:T(8,128)(2,1)}), bf16[16,160,128]{2,1,0:T(8,128)(2,1)S(1)}, u32[]{:S(2)}, u32[]{:S(2)}) async-start(bf16[16,160,128]{2,1,0:T(8,128)(2,1)} %pad_maximum_fusion), calls=%async_computation | async-start | bytes 1310720 | tf_op jit(solution)/shard_map/all_to_all | solution.py:302
  36.7 21.8 %collective-permute-start.6 = (bf16[80,1024]{1,0:T(8,128)(2,1)S(1)}, bf16[80,1024]{1,0:T(8,128)(2,1)S(1)}, u32[]{:S(2)}, u32[]{:S(2)}) collective-permute-start(bf16[80,1024]{1,0:T(8,128)(2,1)S(1)} %slice.56), channel_id=1, source_target_pairs={{0,32},{16,48},{32,64},{48,80},{64,96},{80,112},{96,128},{112,144}... | collective-permute-start | bytes 491528 | tf_op jit(solution)/shard_map/ppermute | solution.py:252
  38.5 6.3 %collective-permute-start.13 = (bf16[160,1024]{1,0:T(8,128)(2,1)S(1)}, bf16[160,1024]{1,0:T(8,128)(2,1)S(1)}, u32[]{:S(2)}, u32[]{:S(2)}) collective-permute-start(bf16[160,1024]{1,0:T(8,128)(2,1)S(1)} %collective-permute-done.5), channel_id=1, source_target_pairs={{0,16},{16,0},{32,48},{48,32},{64,80},{80,64},{96,112},{112,96},{1... | collective-permute-start | bytes 983048 | tf_op jit(solution)/shard_map/ppermute | solution.py:255
  38.5 6.3 %collective-permute-start.14 = (bf16[160,1024]{1,0:T(8,128)(2,1)S(1)}, bf16[160,1024]{1,0:T(8,128)(2,1)S(1)}, u32[]{:S(2)}, u32[]{:S(2)}) collective-permute-start(bf16[160,1024]{1,0:T(8,128)(2,1)S(1)} %collective-permute-done.9), channel_id=1, source_target_pairs={{0,16},{16,0},{32,48},{48,32},{64,80},{80,64},{96,112},{112,96},{1... | collective-permute-start | bytes 983048 | tf_op jit(solution)/shard_map/ppermute | solution.py:255
  41.9 16.5 %collective-permute-start.12 = (bf16[80,1024]{1,0:T(8,128)(2,1)S(1)}, bf16[80,1024]{1,0:T(8,128)(2,1)S(1)}, u32[]{:S(2)}, u32[]{:S(2)}) collective-permute-start(bf16[80,1024]{1,0:T(8,128)(2,1)S(1)} %slice.43), channel_id=1, source_target_pairs={{0,224},{16,240},{32,0},{48,16},{64,32},{80,48},{96,64},{112,80},{... | collective-permute-start | bytes 491528 | tf_op jit(solution)/shard_map/ppermute | solution.py:252
  58.5 1.4 %collective-permute-start.16 = (bf16[80,1024]{1,0:T(8,128)(2,1)S(1)}, bf16[80,1024]{1,0:T(8,128)(2,1)S(1)}, u32[]{:S(2)}, u32[]{:S(2)}) collective-permute-start(bf16[80,1024]{1,0:T(8,128)(2,1)S(1)} %collective-permute-done.12), channel_id=1, source_target_pairs={{0,16},{16,0},{32,48},{48,32},{64,80},{80,64},{96,112},{112,96},{1... | collective-permute-start | bytes 491528 | tf_op jit(solution)/shard_map/ppermute | solution.py:255
  58.5 1.6 %collective-permute-start.15 = (bf16[80,1024]{1,0:T(8,128)(2,1)S(1)}, bf16[80,1024]{1,0:T(8,128)(2,1)S(1)}, u32[]{:S(2)}, u32[]{:S(2)}) collective-permute-start(bf16[80,1024]{1,0:T(8,128)(2,1)S(1)} %collective-permute-done.6), channel_id=1, source_target_pairs={{0,16},{16,0},{32,48},{48,32},{64,80},{80,64},{96,112},{112,96},{1... | collective-permute-start | bytes 491528 | tf_op jit(solution)/shard_map/ppermute | solution.py:255
  72.2 1.3 %collective-permute-start.17 = (f32[4,2560]{1,0:T(4,128)S(1)}, f32[4,2560]{1,0:T(4,128)S(1)}, u32[]{:S(2)}, u32[]{:S(2)}) collective-permute-start(f32[4,2560]{1,0:T(4,128)S(1)} %get-tuple-element.48), channel_id=1, source_target_pairs={{0,16},{16,0},{32,48},{48,32},{64,80},{80,64},{96,112},{112,96},{1... | collective-permute-start | bytes 122888 | tf_op jit(solution)/shard_map/ppermute | solution.py:326
  73.7 4.1 %collective-permute-start.18 = (f32[4,2560]{1,0:T(4,128)S(1)}, f32[4,2560]{1,0:T(4,128)S(1)}, u32[]{:S(2)}, u32[]{:S(2)}) collective-permute-start(f32[4,2560]{1,0:T(4,128)S(1)} %fusion), channel_id=1, source_target_pairs={{0,32},{16,48},{32,0},{48,16},{64,96},{80,112},{96,64},{112,80},{1... | collective-permute-start | bytes 122888 | tf_op jit(solution)/shard_map/ppermute | solution.py:326
  78.0 5.4 %collective-permute-start.19 = (f32[4,2560]{1,0:T(4,128)S(1)}, f32[4,2560]{1,0:T(4,128)S(1)}, u32[]{:S(2)}, u32[]{:S(2)}) collective-permute-start(f32[4,2560]{1,0:T(4,128)S(1)} %fusion.1), channel_id=1, source_target_pairs={{0,64},{16,80},{32,96},{48,112},{64,0},{80,16},{96,32},{112,48},{1... | collective-permute-start | bytes 122888 | tf_op jit(solution)/shard_map/ppermute | solution.py:326
  (2 other events, 1.6 us)

commit v5 on v4

--- a/solution.py
+++ b/solution.py
@@ -285,8 +285,10 @@
     right = left = inputs
     for step in range(1, chips // 2 + 1):
         last = step == chips // 2
+        if step > 2:
+            right, left, feats = lax.optimization_barrier((right, left, feats))
         right = shift(right[:half] if last else right, 1)
-        if step > 1:
+        if step == 2:
             left, feats = lax.optimization_barrier((left, feats))
         left = shift(left[half:] if last else left, -1)
         if step == 2:

time: 110 us -> 109 us (level)
  blocking collectives: 16.2 us -> 14.3 us
  Pallas kernels: 21.6 us -> 23.4 us
  starting transfers between devices: 25.2 us -> 23.9 us
  waiting for transfers between devices: 29.9 us -> 31.2 us
    all_to_all x1, blocking collectives: 16.2 us -> 14.3 us  [body(): lax.all_to_all(part.reshape(n_batch, dim // n_batch, width), 'batch', 0, 0)]
    ppermute x8, waiting for transfers between devices: 20.6 us -> 21.9 us  [shift(): lax.ppermute(x, 'seq', [(a, (a + 2 * by) % n_seq) for a in range(n_seq)])]
    ppermute x8, starting transfers between devices: 17 us -> 15.7 us  [shift(): lax.ppermute(x, 'seq', [(a, (a + 2 * by) % n_seq) for a in range(n_seq)])]
  transfers between devices with their start and end apart: 21 -> 21, of which waited for: 9 -> 9; matrix products, arithmetic and copies ran while one was open for 9% -> 8% of each run, Pallas kernels for 2% -> 2%
where the time goes in v5:
time: 109 us
  waiting for transfers between devices  31.2 us (29%)
  starting transfers between devices  23.9 us (22%)
  Pallas kernels  23.4 us (21%)
  blocking collectives  14.3 us (13%)
  other arithmetic  9.76 us (9%)
  local copies, waits for them, and re-layouts  5.7 us (5%)
    ppermute x8, waiting for transfers between devices, shift(): lax.ppermute(x, 'seq', [(a, (a + 2 * by) % n_seq) for a in range(n_seq)])  21.9 us
    ppermute x8, starting transfers between devices, shift(): lax.ppermute(x, 'seq', [(a, (a + 2 * by) % n_seq) for a in range(n_seq)])  15.7 us
    all_to_all x1, blocking collectives, body(): lax.all_to_all(part.reshape(n_batch, dim // n_batch, width), 'batch', 0, 0)  14.3 us
    pallas_call x1, Pallas kernels, body(): pl.pallas_call(functools.partial(forward_kernel, scale=scale), in_specs=[...  12 us
    pallas_call x1, Pallas kernels, body(): pl.pallas_call(functools.partial(backward_kernel, scale=scale, width=widt...  9.1 us
    ppermute x3, waiting for transfers between devices, body(): other = lax.ppermute(stats, 'seq', [(a, a ^ step) for a in range(n_seq)])  8.22 us
    dynamic_update_slice x7, other arithmetic, place(): lax.dynamic_update_slice(feats, jnp.concatenate(ordered, axis=0), (first,...  6.3 us
    unnamed x11, local copies, waits for them, and re-layouts  4.87 us
  transfers between devices with their start and end apart: 21, of which 9 were waited for; matrix products, arithmetic and copies ran while one was open for 8% of the time, Pallas kernels for 2%

profile of v5, /device:TPU:2, one launch (start us, length us, event | category | flops | bytes accessed | tf_op | source)
XLA Modules:
  0.0 108.6 jit_solution(15235560666019079680)
XLA Ops:
  0.0 5.9 %collective-permute-start.2 = (bf16[160,1024]{1,0:T(8,128)(2,1)}, bf16[160,1024]{1,0:T(8,128)(2,1)S(1)}, u32[]{:S(2)}, u32[]{:S(2)}) collective-permute-start(bf16[160,1024]{1,0:T(8,128)(2,1)} %bitcast.12), channel_id=1, source_target_pairs={{0,224},{16,240},{32,0},{48,16},{64,32},{80,48},{96,64},{112,80},{... | collective-permute-start | bytes 983048 | tf_op jit(solution)/shard_map/ppermute | solution.py:252
  5.9 1.6 %copy-done = bf16[1024,1024]{1,0:T(8,128)(2,1)S(1)} copy-done((bf16[1024,1024]{1,0:T(8,128)(2,1)S(1)}, bf16[1024,1024]{1,0:T(8,128)(2,1)}, u32[]{:S(2)}) %copy-start) | copy-done | bytes 2097176
  7.5 1.6 %copy-done.1 = bf16[1024,1024]{1,0:T(8,128)(2,1)S(1)} copy-done((bf16[1024,1024]{1,0:T(8,128)(2,1)S(1)}, bf16[1024,1024]{1,0:T(8,128)(2,1)}, u32[]{:S(2)}) %copy-start.1) | copy-done | bytes 2097176
  9.0 1.0 copy-done.2
  10.7 2.3 %prepare.1 = (s32[111]{0:T(128)S(1)}, bf16[1024,512]{1,0:T(8,128)(2,1)S(1)}, bf16[2560,1024]{1,0:T(8,128)(2,1)}) custom-call(s32[1,3]{1,0:T(1,128)S(1)} %copy-done.3, bf16[160,1024]{1,0:T(8,128)(2,1)S(1)} %bitcast.14, bf16[1024,2048]{1,0:T(8,128)(2,1)} %wqk_hbm.1, bf16[1024,1024]{1,0:T(8,128)(2,1)S(1)} %copy-done, bf16[1024,1024]{1,0:T(8,128)(2,1)S(1)} %copy-done.1), custom_call_target="tpu_custom_call" | custom-call | bytes 8000000 | tf_op jit(solution)/shard_map/prepare/pallas_call | solution.py:267
  13.8 3.3 %collective-permute-done = bf16[160,1024]{1,0:T(8,128)(2,1)S(1)} collective-permute-done((bf16[160,1024]{1,0:T(8,128)(2,1)}, bf16[160,1024]{1,0:T(8,128)(2,1)S(1)}, u32[]{:S(2)}, u32[]{:S(2)}) %collective-permute-start) | collective-permute-done | bytes 327712 | tf_op jit(solution)/shard_map/ppermute | solution.py:252
  17.1 3.2 %collective-permute-start.4 = (bf16[160,1024]{1,0:T(8,128)(2,1)S(1)}, bf16[160,1024]{1,0:T(8,128)(2,1)S(1)}, u32[]{:S(2)}, u32[]{:S(2)}) collective-permute-start(bf16[160,1024]{1,0:T(8,128)(2,1)S(1)} %collective-permute-done.2), channel_id=1, source_target_pairs={{0,224},{16,240},{32,0},{48,16},{64,32},{80,48},{96,64},{112,80},{... | collective-permute-start | bytes 983048 | tf_op jit(solution)/shard_map/ppermute | solution.py:252
  20.5 0.9 pad_maximum_fusion
  21.9 5.4 %collective-permute-done.1 = bf16[160,1024]{1,0:T(8,128)(2,1)S(1)} collective-permute-done((bf16[160,1024]{1,0:T(8,128)(2,1)S(1)}, bf16[160,1024]{1,0:T(8,128)(2,1)S(1)}, u32[]{:S(2)}, u32[]{:S(2)}) %collective-permute-start.1) | collective-permute-done | bytes 327712 | tf_op jit(solution)/shard_map/ppermute | solution.py:252
  27.4 0.9 maximum_dynamic-update-slice_fusion
  29.3 3.2 %collective-permute-start.8 = (bf16[160,1024]{1,0:T(8,128)(2,1)S(1)}, bf16[160,1024]{1,0:T(8,128)(2,1)S(1)}, u32[]{:S(2)}, u32[]{:S(2)}) collective-permute-start(bf16[160,1024]{1,0:T(8,128)(2,1)S(1)} %collective-permute-done.4), channel_id=1, source_target_pairs={{0,224},{16,240},{32,0},{48,16},{64,32},{80,48},{96,64},{112,80},{... | collective-permute-start | bytes 983048 | tf_op jit(solution)/shard_map/ppermute | solution.py:252
  33.0 3.6 %all-to-all-start = ((bf16[16,160,128]{2,1,0:T(8,128)(2,1)}), bf16[16,160,128]{2,1,0:T(8,128)(2,1)S(1)}, u32[]{:S(2)}, u32[]{:S(2)}) async-start(bf16[16,160,128]{2,1,0:T(8,128)(2,1)} %pad_maximum_fusion), calls=%async_computation | async-start | bytes 1310720 | tf_op jit(solution)/shard_map/all_to_all | solution.py:304
  36.6 2.0 %collective-permute-done.7 = bf16[160,1024]{1,0:T(8,128)(2,1)S(1)} collective-permute-done((bf16[160,1024]{1,0:T(8,128)(2,1)S(1)}, bf16[160,1024]{1,0:T(8,128)(2,1)S(1)}, u32[]{:S(2)}, u32[]{:S(2)}) %collective-permute-start.7) | collective-permute-done | bytes 327712 | tf_op jit(solution)/shard_map/ppermute | solution.py:252
  40.1 1.0 broadcast_select_fusion.5
  41.1 0.9 maximum_dynamic-update-slice_fusion.3
  42.1 3.3 %collective-permute-start.12 = (bf16[80,1024]{1,0:T(8,128)(2,1)S(1)}, bf16[80,1024]{1,0:T(8,128)(2,1)S(1)}, u32[]{:S(2)}, u32[]{:S(2)}) collective-permute-start(bf16[80,1024]{1,0:T(8,128)(2,1)S(1)} %slice.43), channel_id=1, source_target_pairs={{0,224},{16,240},{32,0},{48,16},{64,32},{80,48},{96,64},{112,80},{... | collective-permute-start | bytes 491528 | tf_op jit(solution)/shard_map/ppermute | solution.py:252
  47.3 11.2 %collective-permute-done.11 = bf16[80,1024]{1,0:T(8,128)(2,1)S(1)} collective-permute-done((bf16[80,1024]{1,0:T(8,128)(2,1)S(1)}, bf16[80,1024]{1,0:T(8,128)(2,1)S(1)}, u32[]{:S(2)}, u32[]{:S(2)}) %collective-permute-start.11) | collective-permute-done | bytes 163872 | tf_op jit(solution)/shard_map/ppermute | solution.py:252
  61.1 12.0 %forward.1 = (bf16[2560,128]{1,0:T(8,128)(2,1)S(1)}, bf16[2560,128]{1,0:T(8,128)(2,1)S(1)}, bf16[2560,128]{1,0:T(8,128)(2,1)S(1)}, f32[2560,128]{1,0:T(8,128)S(1...) custom-call(s32[111]{0:T(128)S(1)} %get-tuple-element.29.plan, ...), custom_call_target="tpu_custom_call" | custom-call | flops 12000000000 | bytes 12000000 | tf_op jit(solution)/shard_map/forward/pallas_call | solution.py:310
  73.4 0.9 collective-permute-done.17
  74.9 3.7 %collective-permute-done.18 = f32[4,2560]{1,0:T(4,128)S(1)} collective-permute-done((f32[4,2560]{1,0:T(4,128)S(1)}, f32[4,2560]{1,0:T(4,128)S(1)}, u32[]{:S(2)}, u32[]{:S(2)}) %collective-permute-start.18) | collective-permute-done | bytes 40992 | tf_op jit(solution)/shard_map/ppermute | solution.py:328
  78.8 1.9 %collective-permute-start.19 = (f32[4,2560]{1,0:T(4,128)S(1)}, f32[4,2560]{1,0:T(4,128)S(1)}, u32[]{:S(2)}, u32[]{:S(2)}) collective-permute-start(f32[4,2560]{1,0:T(4,128)S(1)} %fusion.1), channel_id=1, source_target_pairs={{0,64},{16,80},{32,96},{48,112},{64,0},{80,16},{96,32},{112,48},{1... | collective-permute-start | bytes 122888 | tf_op jit(solution)/shard_map/ppermute | solution.py:328
  80.7 3.5 %collective-permute-done.19 = f32[4,2560]{1,0:T(4,128)S(1)} collective-permute-done((f32[4,2560]{1,0:T(4,128)S(1)}, f32[4,2560]{1,0:T(4,128)S(1)}, u32[]{:S(2)}, u32[]{:S(2)}) %collective-permute-start.19) | collective-permute-done | bytes 40992 | tf_op jit(solution)/shard_map/ppermute | solution.py:328
  84.5 9.1 %backward.1 = bf16[128,1024]{1,0:T(8,128)(2,1)S(1)} custom-call(s32[111]{0:T(128)S(1)} %get-tuple-element.29.plan, bf16[2560,1024]{1,0:T(8,128)(2,1)} %maximum_dynamic-update-slice_fusion.6.feats_hbm, bf16[2560,128]{1,0:T(8,128)(2,1)S(1)} %get-tuple-element.46.q_ref, bf16[2560,128]{1,0:T(8,128)(2,1)S(1)} %get-tuple-element.47.k_ref, ...), custom_call_target="tpu_custom_call" | custom-call | tf_op jit(solution)/shard_map/backward/pallas_call | solution.py:335
  93.6 14.3 %all_to_all.10 = bf16[16,8,1024]{2,1,0:T(8,128)(2,1)S(1)} all-to-all(bf16[16,8,1024]{2,1,0:T(8,128)(2,1)S(1)} %bitcast.9), channel_id=1, replica_groups=mesh['seq'=16,'batch'=16] {'batch'}, dimensions={0} | all-to-all | bytes 524288 | tf_op jit(solution)/shard_map/all_to_all | solution.py:350
  (65 shorter events, 11.5 us)
Async XLA Ops:
  0.0 13.0 %collective-permute-start.3 = (bf16[160,1024]{1,0:T(8,128)(2,1)}, bf16[160,1024]{1,0:T(8,128)(2,1)S(1)}, u32[]{:S(2)}, u32[]{:S(2)}) collective-permute-start(bf16[160,1024]{1,0:T(8,128)(2,1)} %bitcast.11), channel_id=1, source_target_pairs={{0,16},{16,0},{32,48},{48,32},{64,80},{80,64},{96,112},{112,96},{1... | collective-permute-start | bytes 983048 | tf_op jit(solution)/shard_map/ppermute | solution.py:255
  0.0 13.8 %collective-permute-start.2 = (bf16[160,1024]{1,0:T(8,128)(2,1)}, bf16[160,1024]{1,0:T(8,128)(2,1)S(1)}, u32[]{:S(2)}, u32[]{:S(2)}) collective-permute-start(bf16[160,1024]{1,0:T(8,128)(2,1)} %bitcast.12), channel_id=1, source_target_pairs={{0,224},{16,240},{32,0},{48,16},{64,32},{80,48},{96,64},{112,80},{... | collective-permute-start | bytes 983048 | tf_op jit(solution)/shard_map/ppermute | solution.py:252
  5.9 11.3 %collective-permute-start = (bf16[160,1024]{1,0:T(8,128)(2,1)}, bf16[160,1024]{1,0:T(8,128)(2,1)S(1)}, u32[]{:S(2)}, u32[]{:S(2)}) collective-permute-start(bf16[160,1024]{1,0:T(8,128)(2,1)} %bitcast.13), channel_id=1, source_target_pairs={{0,32},{16,48},{32,64},{48,80},{64,96},{80,112},{96,128},{112,144}... | collective-permute-start | bytes 983048 | tf_op jit(solution)/shard_map/ppermute | solution.py:252
  5.9 1.6 %copy-start = (bf16[1024,1024]{1,0:T(8,128)(2,1)S(1)}, bf16[1024,1024]{1,0:T(8,128)(2,1)}, u32[]{:S(2)}) copy-start(bf16[1024,1024]{1,0:T(8,128)(2,1)} %wv_hbm.1) | copy-start | bytes 6291460
  7.5 1.6 %copy-start.1 = (bf16[1024,1024]{1,0:T(8,128)(2,1)S(1)}, bf16[1024,1024]{1,0:T(8,128)(2,1)}, u32[]{:S(2)}) copy-start(bf16[1024,1024]{1,0:T(8,128)(2,1)} %wu_hbm.1) | copy-start | bytes 6291460
  10.7 9.7 %copy-start.4 = (bf16[1,160,1024]{2,1,0:T(8,128)(2,1)S(1)}, bf16[1,160,1024]{2,1,0:T(8,128)(2,1)}, u32[]{:S(2)}) copy-start(bf16[1,160,1024]{2,1,0:T(8,128)(2,1)} %param.10) | copy-start | bytes 983044
  17.1 10.2 %collective-permute-start.1 = (bf16[160,1024]{1,0:T(8,128)(2,1)S(1)}, bf16[160,1024]{1,0:T(8,128)(2,1)S(1)}, u32[]{:S(2)}, u32[]{:S(2)}) collective-permute-start(bf16[160,1024]{1,0:T(8,128)(2,1)S(1)} %collective-permute-done), channel_id=1, source_target_pairs={{0,32},{16,48},{32,64},{48,80},{64,96},{80,112},{96,128},{112,144}... | collective-permute-start | bytes 983048 | tf_op jit(solution)/shard_map/ppermute | solution.py:252
  17.1 10.2 %collective-permute-start.4 = (bf16[160,1024]{1,0:T(8,128)(2,1)S(1)}, bf16[160,1024]{1,0:T(8,128)(2,1)S(1)}, u32[]{:S(2)}, u32[]{:S(2)}) collective-permute-start(bf16[160,1024]{1,0:T(8,128)(2,1)S(1)} %collective-permute-done.2), channel_id=1, source_target_pairs={{0,224},{16,240},{32,0},{48,16},{64,32},{80,48},{96,64},{112,80},{... | collective-permute-start | bytes 983048 | tf_op jit(solution)/shard_map/ppermute | solution.py:252
  20.4 7.0 %collective-permute-start.5 = (bf16[160,1024]{1,0:T(8,128)(2,1)S(1)}, bf16[160,1024]{1,0:T(8,128)(2,1)S(1)}, u32[]{:S(2)}, u32[]{:S(2)}) collective-permute-start(bf16[160,1024]{1,0:T(8,128)(2,1)S(1)} %collective-permute-done), channel_id=1, source_target_pairs={{0,16},{16,0},{32,48},{48,32},{64,80},{80,64},{96,112},{112,96},{1... | collective-permute-start | bytes 983048 | tf_op jit(solution)/shard_map/ppermute | solution.py:255
  21.4 6.9 %collective-permute-start.6 = (bf16[160,1024]{1,0:T(8,128)(2,1)S(1)}, bf16[160,1024]{1,0:T(8,128)(2,1)S(1)}, u32[]{:S(2)}, u32[]{:S(2)}) collective-permute-start(bf16[160,1024]{1,0:T(8,128)(2,1)S(1)} %collective-permute-done.2), channel_id=1, source_target_pairs={{0,16},{16,0},{32,48},{48,32},{64,80},{80,64},{96,112},{112,96},{1... | collective-permute-start | bytes 983048 | tf_op jit(solution)/shard_map/ppermute | solution.py:255
  29.3 9.3 %collective-permute-start.7 = (bf16[160,1024]{1,0:T(8,128)(2,1)S(1)}, bf16[160,1024]{1,0:T(8,128)(2,1)S(1)}, u32[]{:S(2)}, u32[]{:S(2)}) collective-permute-start(bf16[160,1024]{1,0:T(8,128)(2,1)S(1)} %collective-permute-done.1), channel_id=1, source_target_pairs={{0,32},{16,48},{32,64},{48,80},{64,96},{80,112},{96,128},{112,144}... | collective-permute-start | bytes 983048 | tf_op jit(solution)/shard_map/ppermute | solution.py:252
  29.3 9.3 %collective-permute-start.8 = (bf16[160,1024]{1,0:T(8,128)(2,1)S(1)}, bf16[160,1024]{1,0:T(8,128)(2,1)S(1)}, u32[]{:S(2)}, u32[]{:S(2)}) collective-permute-start(bf16[160,1024]{1,0:T(8,128)(2,1)S(1)} %collective-permute-done.4), channel_id=1, source_target_pairs={{0,224},{16,240},{32,0},{48,16},{64,32},{80,48},{96,64},{112,80},{... | collective-permute-start | bytes 983048 | tf_op jit(solution)/shard_map/ppermute | solution.py:252
  32.5 6.6 %collective-permute-start.9 = (bf16[160,1024]{1,0:T(8,128)(2,1)S(1)}, bf16[160,1024]{1,0:T(8,128)(2,1)S(1)}, u32[]{:S(2)}, u32[]{:S(2)}) collective-permute-start(bf16[160,1024]{1,0:T(8,128)(2,1)S(1)} %collective-permute-done.1), channel_id=1, source_target_pairs={{0,16},{16,0},{32,48},{48,32},{64,80},{80,64},{96,112},{112,96},{1... | collective-permute-start | bytes 983048 | tf_op jit(solution)/shard_map/ppermute | solution.py:255
  32.5 7.5 %collective-permute-start.10 = (bf16[160,1024]{1,0:T(8,128)(2,1)S(1)}, bf16[160,1024]{1,0:T(8,128)(2,1)}, u32[]{:S(2)}, u32[]{:S(2)}) collective-permute-start(bf16[160,1024]{1,0:T(8,128)(2,1)S(1)} %collective-permute-done.4), channel_id=1, source_target_pairs={{0,16},{16,0},{32,48},{48,32},{64,80},{80,64},{96,112},{112,96},{1... | collective-permute-start | bytes 983048 | tf_op jit(solution)/shard_map/ppermute | solution.py:255
  33.0 28.0 %all-to-all-start = ((bf16[16,160,128]{2,1,0:T(8,128)(2,1)}), bf16[16,160,128]{2,1,0:T(8,128)(2,1)S(1)}, u32[]{:S(2)}, u32[]{:S(2)}) async-start(bf16[16,160,128]{2,1,0:T(8,128)(2,1)} %pad_maximum_fusion), calls=%async_computation | async-start | bytes 1310720 | tf_op jit(solution)/shard_map/all_to_all | solution.py:304
  38.6 6.8 %collective-permute-start.13 = (bf16[160,1024]{1,0:T(8,128)(2,1)S(1)}, bf16[160,1024]{1,0:T(8,128)(2,1)S(1)}, u32[]{:S(2)}, u32[]{:S(2)}) collective-permute-start(bf16[160,1024]{1,0:T(8,128)(2,1)S(1)} %collective-permute-done.7), channel_id=1, source_target_pairs={{0,16},{16,0},{32,48},{48,32},{64,80},{80,64},{96,112},{112,96},{1... | collective-permute-start | bytes 983048 | tf_op jit(solution)/shard_map/ppermute | solution.py:255
  38.6 6.9 %collective-permute-start.14 = (bf16[160,1024]{1,0:T(8,128)(2,1)S(1)}, bf16[160,1024]{1,0:T(8,128)(2,1)S(1)}, u32[]{:S(2)}, u32[]{:S(2)}) collective-permute-start(bf16[160,1024]{1,0:T(8,128)(2,1)S(1)} %collective-permute-done.8), channel_id=1, source_target_pairs={{0,16},{16,0},{32,48},{48,32},{64,80},{80,64},{96,112},{112,96},{1... | collective-permute-start | bytes 983048 | tf_op jit(solution)/shard_map/ppermute | solution.py:255
  42.0 16.5 %collective-permute-start.11 = (bf16[80,1024]{1,0:T(8,128)(2,1)S(1)}, bf16[80,1024]{1,0:T(8,128)(2,1)S(1)}, u32[]{:S(2)}, u32[]{:S(2)}) collective-permute-start(bf16[80,1024]{1,0:T(8,128)(2,1)S(1)} %slice.42), channel_id=1, source_target_pairs={{0,32},{16,48},{32,64},{48,80},{64,96},{80,112},{96,128},{112,144}... | collective-permute-start | bytes 491528 | tf_op jit(solution)/shard_map/ppermute | solution.py:252
  42.1 16.4 %collective-permute-start.12 = (bf16[80,1024]{1,0:T(8,128)(2,1)S(1)}, bf16[80,1024]{1,0:T(8,128)(2,1)S(1)}, u32[]{:S(2)}, u32[]{:S(2)}) collective-permute-start(bf16[80,1024]{1,0:T(8,128)(2,1)S(1)} %slice.43), channel_id=1, source_target_pairs={{0,224},{16,240},{32,0},{48,16},{64,32},{80,48},{96,64},{112,80},{... | collective-permute-start | bytes 491528 | tf_op jit(solution)/shard_map/ppermute | solution.py:252
  58.5 1.4 %collective-permute-start.16 = (bf16[80,1024]{1,0:T(8,128)(2,1)S(1)}, bf16[80,1024]{1,0:T(8,128)(2,1)S(1)}, u32[]{:S(2)}, u32[]{:S(2)}) collective-permute-start(bf16[80,1024]{1,0:T(8,128)(2,1)S(1)} %collective-permute-done.12), channel_id=1, source_target_pairs={{0,16},{16,0},{32,48},{48,32},{64,80},{80,64},{96,112},{112,96},{1... | collective-permute-start | bytes 491528 | tf_op jit(solution)/shard_map/ppermute | solution.py:255
  58.5 1.6 %collective-permute-start.15 = (bf16[80,1024]{1,0:T(8,128)(2,1)S(1)}, bf16[80,1024]{1,0:T(8,128)(2,1)S(1)}, u32[]{:S(2)}, u32[]{:S(2)}) collective-permute-start(bf16[80,1024]{1,0:T(8,128)(2,1)S(1)} %collective-permute-done.11), channel_id=1, source_target_pairs={{0,16},{16,0},{32,48},{48,32},{64,80},{80,64},{96,112},{112,96},{1... | collective-permute-start | bytes 491528 | tf_op jit(solution)/shard_map/ppermute | solution.py:255
  73.0 1.3 %collective-permute-start.17 = (f32[4,2560]{1,0:T(4,128)S(1)}, f32[4,2560]{1,0:T(4,128)S(1)}, u32[]{:S(2)}, u32[]{:S(2)}) collective-permute-start(f32[4,2560]{1,0:T(4,128)S(1)} %get-tuple-element.52), channel_id=1, source_target_pairs={{0,16},{16,0},{32,48},{48,32},{64,80},{80,64},{96,112},{112,96},{1... | collective-permute-start | bytes 122888 | tf_op jit(solution)/shard_map/ppermute | solution.py:328
  74.5 4.1 %collective-permute-start.18 = (f32[4,2560]{1,0:T(4,128)S(1)}, f32[4,2560]{1,0:T(4,128)S(1)}, u32[]{:S(2)}, u32[]{:S(2)}) collective-permute-start(f32[4,2560]{1,0:T(4,128)S(1)} %fusion), channel_id=1, source_target_pairs={{0,32},{16,48},{32,0},{48,16},{64,96},{80,112},{96,64},{112,80},{1... | collective-permute-start | bytes 122888 | tf_op jit(solution)/shard_map/ppermute | solution.py:328
  78.8 5.4 %collective-permute-start.19 = (f32[4,2560]{1,0:T(4,128)S(1)}, f32[4,2560]{1,0:T(4,128)S(1)}, u32[]{:S(2)}, u32[]{:S(2)}) collective-permute-start(f32[4,2560]{1,0:T(4,128)S(1)} %fusion.1), channel_id=1, source_target_pairs={{0,64},{16,80},{32,96},{48,112},{64,0},{80,16},{96,32},{112,48},{1... | collective-permute-start | bytes 122888 | tf_op jit(solution)/shard_map/ppermute | solution.py:328
  (2 other events, 1.6 us)
